TPU v7x, 32 devices: a whole 2x2x4 slice. The times are simulated.
32 devices in a mesh: req: 8 (over y, x, core), tp: 4 (over z).
Axes of the slice: x: 2, y: 2, z: 4, core: 2. Of those that a mesh axis runs over, the one named last changes fastest.
Arguments:
- activations: bfloat16 [2048, 2304], P('req'), may hold values from -6 to 6
- lengths: int32 [8, 4], P('req'), may hold values from 1 to 192, 256 in all within a row
- adapter_of: int32 [8, 4], P('req'), may hold values from 0 to 15
- slot_of: int32 [16], replicated, may hold values from 0 to 15, as said below
- page_table: int32 [8, 6], P('req'), may hold values from 0 to 5, each once within a row
- experts_of: int32 [2048, 2], P('req'), may hold values from 0 to 7, all different within a row; in each aligned block of 256 rows (0 to 255, 256 to 511, ...) at most 72 rows name the same one
- attn_gain: float32 [2304], replicated, may hold values from 0.25 to 1.75
- moe_gain: float32 [2304], replicated, may hold values from 0.25 to 1.75
- w_qkv: bfloat16 [2304, 3, 2304], P(None, None, 'tp'), may hold values from -4 to 4
- output_weight: bfloat16 [2304, 2304], P('tp'), may hold values from -0.125 to 0.125
- router: bfloat16 [2304, 8], replicated, may hold values from -0.125 to 0.125
- w_gate_up: bfloat16 [8, 2304, 2, 5760], P('req', None, None, 'tp'), may hold values from -0.125 to 0.125
- w_down: bfloat16 [8, 5760, 2304], P('req', 'tp'), may hold values from -0.078125 to 0.078125
- expert_up_factors: bfloat16 [8, 256, 2, 5760], P('req', None, None, 'tp'), may hold values from -0.59765625 to 0.59765625
- pool_a: bfloat16 [16, 2304, 64], P('req'), may hold values from -0.125 to 0.125
- slot_query_key_value_up: bfloat16 [16, 16, 3, 2304], P('req', None, None, 'tp'), may hold values from -0.59765625 to 0.59765625
- pool_aout: bfloat16 [16, 2304, 16], P('req', 'tp'), may hold values from -0.125 to 0.125
- pool_bout: bfloat16 [16, 16, 2304], P('req'), may hold values from -1.796875 to 1.796875
Outputs:
- layer_out: bfloat16 [2048, 2304], P('req')
- page_cache: bfloat16 [48, 128, 2, 2304], P('req', None, None, 'tp')
Inputs may be any that keep to these rules, and one draw needn't show every extreme that they name: `slot_of`: distinct slots. `page_table`: each row holds every page index once. `experts_of`: the two experts of a token differ; among the 256 tokens of one index of req at most 72 choose one expert, and some expert reaches 72.
All inputs are finite; a program needn't handle non-finite values.
Results may differ from a plain program's by a relative error of at most 0.0095.
Values may be sent and summed in bfloat16 or wider, within the bound.
A program may use at most 128 MiB of HBM per device.

v0:
```python
import math

import jax
import jax.numpy as jnp
from jax import lax
from jax.sharding import PartitionSpec as P

D = 2304
HEAD_SIZE = 64
EXPERTS = 8
ADAPTER_RANK = 16
ADAPTER_TOTAL = 16
PAGE = 128
CAP = 72


epsilon = 1e-05
adapter_scale = 2.0
rope_base = 10000.0


def rms_norm(values, scales):
    mean_sq = jnp.mean(values * values, axis=-1, keepdims=True)
    return values * lax.rsqrt(mean_sq + epsilon) * scales


def token_layout(lengths_row, tok_count):
    ends_at = jnp.cumsum(lengths_row)
    starts = ends_at - lengths_row
    places = jnp.arange(tok_count, dtype=jnp.int32)
    request = jnp.sum((places[:, None] >= ends_at[None, :]).astype(jnp.int32), axis=1)
    position = places - starts[request]
    return (request, position)


def rotate(values, position):
    head_dim = values.shape[-1]
    half_dim = head_dim // 2
    frequency = rope_base ** (-jnp.arange(half_dim, dtype=jnp.float32) * 2.0 / head_dim)
    angles = position.astype(jnp.float32)[:, None] * frequency[None, :]
    cosine = jnp.cos(angles)[:, None, :]
    sine_part = jnp.sin(angles)[:, None, :]
    front_half = values[..., :half_dim]
    back_half = values[..., half_dim:]
    return jnp.concatenate(
        [front_half * cosine - back_half * sine_part, back_half * cosine + front_half * sine_part],
        axis=-1,
    )


def per_device(
    activations,
    lengths,
    adapter_of,
    slot_of,
    page_table,
    experts_of,
    attn_gain,
    moe_gain,
    w_qkv,
    output_weight,
    router,
    w_gate_up,
    w_down,
    expert_up_factors,
    pool_a,
    slot_query_key_value_up,
    pool_aout,
    pool_bout,
):
    token_share = activations.shape[0]
    n_req = lax.axis_size("req")
    request, position = token_layout(lengths[0], token_share)
    adapter = adapter_of[0][request]
    token_slot = slot_of[adapter]
    pool_down, slot_up_factors, pool_head, pool_outup = (
        lax.all_gather(pool_a, "req", axis=0, tiled=True),
        lax.all_gather(slot_query_key_value_up, "req", axis=0, tiled=True),
        lax.all_gather(pool_aout, "req", axis=0, tiled=True),
        lax.all_gather(pool_bout, "req", axis=0, tiled=True),
    )
    slot_count = pool_down.shape[0]
    slot_hot = token_slot[:, None] == jnp.arange(slot_count, dtype=jnp.int32)[None, :]
    head_width = w_qkv.shape[2]
    heads_number = head_width // HEAD_SIZE
    normed = rms_norm(activations.astype(jnp.float32), attn_gain).astype(jnp.bfloat16)
    down_all = jnp.einsum(
        "td,sdr->tsr",
        normed,
        pool_down[:, :, : 3 * ADAPTER_RANK],
        preferred_element_type=jnp.float32,
    )
    coeff_qkv = jnp.sum(jnp.where(slot_hot[:, :, None], down_all, 0.0), axis=1).astype(jnp.bfloat16)
    spread_rows = jnp.where(
        slot_hot[:, :, None, None],
        coeff_qkv.reshape(token_share, 1, 3, ADAPTER_RANK),
        jnp.zeros((), jnp.bfloat16),
    )
    adapter_query_key_value = jnp.einsum(
        "qwxv,wvxd->qxd", spread_rows, slot_up_factors, preferred_element_type=jnp.float32
    )
    plain_query_key_value = jnp.dot(
        normed, w_qkv.reshape(D, 3 * head_width), preferred_element_type=jnp.float32
    ).reshape(token_share, 3, head_width)
    projection_result = (plain_query_key_value + adapter_scale * adapter_query_key_value).reshape(
        token_share, 3, heads_number, HEAD_SIZE
    )
    queries = rotate(projection_result[:, 0], position).astype(jnp.bfloat16)
    keys_roped = rotate(projection_result[:, 1], position).astype(jnp.bfloat16)
    values = projection_result[:, 2].astype(jnp.bfloat16)
    pool_dev = page_table.shape[1]
    pages_used = (lengths[0] + PAGE - 1) // PAGE
    first_page = jnp.cumsum(pages_used) - pages_used
    local_page = page_table[0][first_page[request] + position // PAGE]
    cache_row = local_page * PAGE + position % PAGE
    place_hot = (
        jnp.arange(pool_dev * PAGE, dtype=jnp.int32)[:, None] == cache_row[None, :]
    ).astype(jnp.bfloat16)
    key_value = jnp.stack(
        [keys_roped.reshape(token_share, head_width), values.reshape(token_share, head_width)],
        axis=1,
    ).reshape(token_share, 2 * head_width)
    page_cache = (
        jnp.dot(place_hot, key_value, preferred_element_type=jnp.float32)
        .astype(jnp.bfloat16)
        .reshape(pool_dev, PAGE, 2, head_width)
    )
    scores = jnp.einsum("qhd,khd->hqk", queries, keys_roped, preferred_element_type=jnp.float32) * (
        1.0 / math.sqrt(HEAD_SIZE)
    )
    allowed = (request[:, None] == request[None, :]) & (position[None, :] <= position[:, None])
    scores = jnp.where(allowed[None], scores, -1e30)
    row_max = jnp.max(scores, axis=-1, keepdims=True)
    weights = jnp.exp(scores - row_max)
    weights = (weights / jnp.sum(weights, axis=-1, keepdims=True)).astype(jnp.bfloat16)
    attention_result = (
        jnp.einsum("hqk,khd->qhd", weights, values, preferred_element_type=jnp.float32)
        .astype(jnp.bfloat16)
        .reshape(token_share, head_width)
    )
    aout_all = jnp.einsum(
        "tc,scr->tsr", attention_result, pool_head, preferred_element_type=jnp.float32
    )
    coeff_out = jnp.sum(jnp.where(slot_hot[:, :, None], aout_all, 0.0), axis=1)
    spread_out = jnp.where(slot_hot[:, :, None], coeff_out[:, None, :], 0.0).reshape(
        token_share, slot_count * ADAPTER_RANK
    )
    output_update = jnp.dot(
        spread_out,
        pool_outup.astype(jnp.float32).reshape(slot_count * ADAPTER_RANK, D),
        precision=lax.Precision.HIGHEST,
    )
    head_term = (
        jnp.dot(attention_result, output_weight, preferred_element_type=jnp.float32)
        + adapter_scale * output_update
    )
    mixed_out = lax.psum(head_term, "tp")
    residual_stream = activations.astype(jnp.float32) + mixed_out
    normed_moe = rms_norm(residual_stream, moe_gain).astype(jnp.bfloat16)
    logits = jnp.dot(normed_moe, router, preferred_element_type=jnp.float32)
    chosen = jnp.take_along_axis(logits, experts_of, axis=1)
    gate_weights = 1.0 / (1.0 + jnp.exp(chosen[:, ::-1] - chosen))
    exp_all = jnp.einsum(
        "td,sdr->tsr",
        normed_moe,
        pool_down[:, :, 3 * ADAPTER_RANK :],
        preferred_element_type=jnp.float32,
    )
    coeff_exp = jnp.sum(jnp.where(slot_hot[:, :, None], exp_all, 0.0), axis=1).astype(jnp.bfloat16)
    capacity = CAP
    split_count = n_req // EXPERTS
    flat_expert = experts_of.reshape(-1)
    expert_hot = (flat_expert[:, None] == jnp.arange(EXPERTS, dtype=jnp.int32)[None, :]).astype(
        jnp.int32
    )
    order_in = jnp.sum((jnp.cumsum(expert_hot, axis=0) - expert_hot) * expert_hot, axis=1)
    column = flat_expert * capacity + order_in
    pick = (column[:, None] == jnp.arange(EXPERTS * capacity, dtype=jnp.int32)[None, :]).reshape(
        token_share, 2, EXPERTS * capacity
    )
    route = jnp.any(pick, axis=1).astype(jnp.bfloat16)
    combine_weights = jnp.sum(jnp.where(pick, gate_weights[:, :, None], 0.0), axis=1)

    def spread_copies(array):
        shaped = array.reshape((EXPERTS, 1, capacity) + array.shape[1:])
        return jnp.broadcast_to(shaped, (EXPERTS, split_count, capacity) + array.shape[1:]).reshape(
            (n_req, capacity) + array.shape[1:]
        )

    send_coeff = jnp.einsum(
        "ts,tr->sr", route, coeff_exp, preferred_element_type=jnp.float32
    ).astype(jnp.bfloat16)
    send_ids = jnp.einsum(
        "ts,t->s", route, adapter.astype(jnp.bfloat16), preferred_element_type=jnp.float32
    ).astype(jnp.bfloat16)
    adapter_range = jnp.arange(ADAPTER_TOTAL, dtype=jnp.int32).astype(jnp.bfloat16)
    send_rows = jnp.einsum(
        "ts,td->sd", route, normed_moe, preferred_element_type=jnp.float32
    ).astype(jnp.bfloat16)
    expert_input_rows = lax.all_to_all(
        spread_copies(send_rows), "req", split_axis=0, concat_axis=0, tiled=True
    )
    coeff_rank = lax.all_to_all(
        spread_copies(send_coeff), "req", split_axis=0, concat_axis=0, tiled=True
    )
    adapter_ids = lax.all_to_all(
        spread_copies(send_ids), "req", split_axis=0, concat_axis=0, tiled=True
    )
    count = expert_input_rows.shape[1]
    flat_rows = expert_input_rows.reshape(n_req * count, D)
    flat_coeff = coeff_rank.reshape(n_req * count, ADAPTER_RANK)
    flat_ids = adapter_ids.reshape(n_req * count)
    unit_count = w_gate_up.shape[3]
    broad_coefficients = jnp.where(
        flat_ids[:, None, None] == adapter_range[None, :, None],
        flat_coeff[:, None, :],
        jnp.zeros((), jnp.bfloat16),
    ).reshape(n_req * count, ADAPTER_TOTAL * ADAPTER_RANK)
    before_norm = jnp.dot(
        flat_rows, w_gate_up[0].reshape(D, 2 * unit_count), preferred_element_type=jnp.float32
    )
    before_norm = before_norm + adapter_scale * jnp.dot(
        broad_coefficients,
        expert_up_factors[0].reshape(ADAPTER_TOTAL * ADAPTER_RANK, 2 * unit_count),
        preferred_element_type=jnp.float32,
    )
    hidden = (jax.nn.silu(before_norm[:, :unit_count]) * before_norm[:, unit_count:]).astype(
        jnp.bfloat16
    )
    partial_term = jnp.dot(hidden, w_down[0], preferred_element_type=jnp.float32).astype(
        jnp.bfloat16
    )
    returned = lax.all_to_all(
        partial_term.reshape(n_req, count, D), "req", split_axis=0, concat_axis=0, tiled=True
    )
    summed = jnp.sum(
        returned.astype(jnp.float32).reshape(EXPERTS, split_count, capacity, D), axis=1
    ).reshape(EXPERTS * capacity, D)
    moe_part = jnp.dot(combine_weights, summed, precision=lax.Precision.HIGHEST)
    moe_sum = lax.psum(moe_part.astype(jnp.bfloat16), "tp").astype(jnp.float32)
    layer_out = (residual_stream + moe_sum).astype(jnp.bfloat16)
    return (layer_out, page_cache)


def solution(mesh):
    return jax.shard_map(
        per_device,
        mesh=mesh,
        in_specs=(
            P("req", None),
            P("req", None),
            P("req", None),
            P(),
            P("req", None),
            P("req", None),
            P(),
            P(),
            P(None, None, "tp"),
            P("tp", None),
            P(),
            P("req", None, None, "tp"),
            P("req", "tp", None),
            P("req", None, None, "tp"),
            P("req", None, None),
            P("req", None, None, "tp"),
            P("req", "tp", None),
            P("req", None, None),
        ),
        out_specs=(P("req", None), P("req", None, None, "tp")),
        check_vma=False,
    )
```

profile of v0, /device:TPU:0, one launch (start us, length us, event | category | flops | bytes accessed | tf_op | source)
XLA Modules:
  0.0 364.0 jit_solution(4491412793175182737)
XLA Ops:
  17.8 6.8 %compare_select_fusion.9 = (s32[256,1]{0,1:T(1,128)S(1)}, s32[256,1]{0,1:T(1,128)S(1)}, s32[256,1]{0,1:T(1,128)S(1)}) fusion(s32[]{:T(128)} %bitcast.20, s32[]{:T(128)} %bitcast.21, s32[]{:T(128)} %bitcast.22, s32[]{:T(128)} %bitcast.23, s32[]{:T(128)} %bitcast.24, s32[]{:T(128)} %bitcast.26, s32[]{:T(128)} %bitcast.25, s32[]{:T(128)} %bitcast.10, ...), kind=kLoop, calls=%fused_computation.105 | loop fusion | flops 6144 | bytes 4140 | tf_op jit(solution)/shard_map/gather | solution.py:75
  24.6 5.7 %select_select_fusion.2 = s32[256]{0:T(256)S(1)} fusion(pred[256]{0:T(512)(128)(4,1)S(1)} %get-tuple-element.22, pred[256]{0:T(512)(128)(4,1)S(1)} %get-tuple-element.21, pred[256]{0:T(512)(128)(4,1)S(1)} %get-tuple-element.20, pred[256]{0:T(512)(128)(4,1)S(1)} %get-tuple-element.19, pred[256]{0:T(512)(128)(4,1)S(1)} %get-tuple-element.18, ...), kind=kLoop, calls=%fused_computation.137 | loop fusion | flops 2304 | bytes 4388 | tf_op jit(solution)/shard_map/gather | solution.py:75
  31.0 8.8 %fusion.49 = (s32[256,1]{0,1:T(1,128)S(1)}, s32[256,1]{0,1:T(1,128)S(1)}) fusion(s32[]{:T(128)} %bitcast.71, s32[]{:T(128)} %bitcast.72, s32[]{:T(128)} %bitcast.73, s32[]{:T(128)} %bitcast.67, s32[]{:T(128)} %bitcast.74, s32[]{:T(128)} %bitcast.68, s32[]{:T(128)} %bitcast.76, s32[]{:T(128)} %bitcast.75, s32[]{:T(128)} %bitcast.70, s32[]{:T(128)} %bitcast.69, ...), kind=kLoop, calls=%fused_computation.132 | loop fusion | flops 11008 | bytes 3128 | tf_op jit(solution)/shard_map/mul | solution.py:115
  40.0 12.0 %all_gather.14 = bf16[16,576,16]{1,2,0:T(8,128)(2,1)S(1)} all-gather(bf16[2,576,16]{1,2,0:T(8,128)(2,1)} %param.34), channel_id=1, replica_groups=mesh['req'=8,'tp'=4] {'req'}, dimensions={0}, use_global_device_ids=true | all-gather | bytes 331776 | tf_op jit(solution)/shard_map/all_gather | solution.py:79
  52.0 12.0 %all_gather.13 = bf16[16,16,3,576]{3,1,2,0:T(8,128)(2,1)} all-gather(bf16[2,16,3,576]{3,1,2,0:T(8,128)(2,1)S(1)} %copy-done.14), channel_id=1, replica_groups=mesh['req'=8,'tp'=4] {'req'}, dimensions={0}, use_global_device_ids=true | all-gather | bytes 995328 | tf_op jit(solution)/shard_map/all_gather | solution.py:78
  64.2 6.8 %fusion.1 = f32[256,3,576]{0,2,1:T(8,128)} fusion(bf16[2304,3,576]{0,2,1:T(8,128)(2,1)} %param.26, bf16[256,2304]{1,0:T(8,128)(2,1)S(1)} %copy-done.5, f32[2304]{0:T(1024)S(1)} %copy-done.18, f32[256]{0:T(256)S(1)} %add_rsqrt_fusion.1), kind=kOutput, calls=%fused_computation.2 | convolution fusion | flops 2040791040 | bytes 10921984 | tf_op jit(solution)/shard_map/dot_general | solution.py:102
  78.1 3.4 fusion.67
  86.5 2.6 convolution_add_fusion
  93.1 3.4 all-to-all-start.1
  96.6 88.4 %all-reduce.3.cloned.1.call-done = f32[256,2304]{1,0:T(8,128)} async-done(((f32[256,2304]{1,0:T(8,128)}), f32[256,2304]{1,0:T(8,128)}) %all-reduce.3.cloned.1.call-update) | async-done | bytes 2359312 | tf_op jit(solution)/shard_map/psum | solution.py:157
  190.9 3.7 %all-to-all-start.2 = ((bf16[8,72,16]{1,2,0:T(8,128)(2,1)}), bf16[8,72,16]{1,2,0:T(8,128)(2,1)S(1)}, u32[]{:S(2)}, u32[]{:S(2)}) async-start(bf16[8,72,16]{1,2,0:T(8,128)(2,1)} %copy.92), calls=%async_computation.2 | async-start | bytes 65536 | tf_op jit(solution)/shard_map/all_to_all | solution.py:203
  194.6 3.7 %convolution_convert_fusion = bf16[576,2304]{1,0:T(8,128)(2,1)} fusion(pred[256,576]{0,1:T(8,128)(4,1)S(1)} %fusion.17, bf16[256,2304]{1,0:T(8,128)(2,1)} %copy-done.3), kind=kOutput, calls=%fused_computation.8 | convolution fusion | flops 680804352 | bytes 3981312 | tf_op jit(solution)/shard_map/ts,td->sd/dot_general | solution.py:197
  199.4 3.6 all-to-all-start
  203.5 32.1 %all-to-all-done = bf16[8,72,2304]{2,1,0:T(8,128)(2,1)S(1)} async-done(((bf16[8,72,2304]{2,1,0:T(8,128)(2,1)}), bf16[8,72,2304]{2,1,0:T(8,128)(2,1)S(1)}, u32[]{:S(2)}, u32[]{:S(2)}) %all-to-all-start) | async-done | bytes 2654240 | tf_op jit(solution)/shard_map/all_to_all | solution.py:200
  235.6 11.4 %fusion.72 = f32[576,2880]{1,0:T(8,128)S(1)} fusion(bf16[576,2304]{1,0:T(8,128)(2,1)S(1)} %bitcast.153, bf16[2304,2880]{0,1:T(8,128)(2,1)} %bitcast.173), kind=kOutput, calls=%fused_computation.165 | convolution fusion | flops 7644119040 | bytes 22560768 | tf_op jit(solution)/shard_map/dot_general | solution.py:219
  248.3 9.2 %fusion.5 = bf16[576,2304]{1,0:T(8,128)(2,1)} fusion(bf16[1,1440,2304]{2,1,0:T(8,128)(2,1)} %param.30, f32[576,2880]{1,0:T(8,128)S(1)} %multiply_add_fusion), kind=kOutput, calls=%fused_computation.7 | convolution fusion | flops 3828363264 | bytes 16367616 | tf_op jit(solution)/shard_map/dot_general | solution.py:230
  257.5 4.5 %all-to-all-start.3 = ((bf16[8,72,2304]{2,1,0:T(8,128)(2,1)}), bf16[8,72,2304]{2,1,0:T(8,128)(2,1)}, u32[]{:S(2)}, u32[]{:S(2)}) async-start(bf16[8,72,2304]{2,1,0:T(8,128)(2,1)} %bitcast.152), calls=%async_computation.3 | async-start | bytes 5308416 | tf_op jit(solution)/shard_map/all_to_all | solution.py:233
  263.0 3.6 gather_fusion
  267.1 27.5 %all-to-all-done.3 = bf16[8,72,2304]{2,1,0:T(8,128)(2,1)} async-done(((bf16[8,72,2304]{2,1,0:T(8,128)(2,1)}), bf16[8,72,2304]{2,1,0:T(8,128)(2,1)}, u32[]{:S(2)}, u32[]{:S(2)}) %all-to-all-start.3) | async-done | bytes 2654240 | tf_op jit(solution)/shard_map/all_to_all | solution.py:233
  294.6 5.9 %convolution_convert_fusion.1 = bf16[256,2304]{1,0:T(8,128)(2,1)} fusion(f32[256,576]{0,1:T(8,128)S(1)} %select_reduce_fusion, bf16[576,2304]{1,0:T(8,128)(2,1)} %bitcast.65), kind=kOutput, calls=%fused_computation.12 | convolution fusion | flops 4077453312 | bytes 4423680 | tf_op jit(solution)/shard_map/dot_general | solution.py:239
  302.5 3.0 reshape.581
  305.5 6.7 %copy.94 = bf16[6,128,2,576]{1,3,2,0:T(8,128)(2,1)} copy(bf16[6,128,2,576]{3,2,1,0:T(2,128)(2,1)} %reshape.581) | data formatting | bytes 3538944
  312.2 41.7 %all-reduce.5.cloned.1.call-done = bf16[256,2304]{1,0:T(8,128)(2,1)} async-done(((bf16[256,2304]{1,0:T(8,128)(2,1)}), bf16[256,2304]{1,0:T(8,128)(2,1)}) %all-reduce.5.cloned.1.call-update) | async-done | bytes 1179664 | tf_op jit(solution)/shard_map/psum | solution.py:240
  353.8 3.7 %add_convert_fusion = bf16[256,2304]{1,0:T(8,128)(2,1)} fusion(bf16[256,2304]{1,0:T(8,128)(2,1)} %all-reduce.5.cloned.1.call-done, f32[256,2304]{1,0:T(8,128)} %all-reduce.3.cloned.1.call-done, bf16[256,2304]{1,0:T(8,128)(2,1)} %param.18), kind=kLoop, calls=%fused_computation.22 | loop fusion | flops 2949120 | bytes 5898240 | tf_op jit(solution)/shard_map/convert_element_type | solution.py:241
  (126 shorter events, 39.8 us)
Async XLA Ops:
  7.2 79.4 %copy-start = (bf16[576,2304]{1,0:T(8,128)(2,1)S(1)}, bf16[576,2304]{1,0:T(8,128)(2,1)}, u32[]{:S(2)}) copy-start(bf16[576,2304]{1,0:T(8,128)(2,1)} %param.27) | copy-start | bytes 7962628
  7.2 44.8 %copy-start.14 = (bf16[2,16,3,576]{3,1,2,0:T(8,128)(2,1)S(1)}, bf16[2,16,3,576]{3,1,2,0:T(8,128)(2,1)}, u32[]{:S(2)}) copy-start(bf16[2,16,3,576]{3,1,2,0:T(8,128)(2,1)} %param.33) | copy-start | bytes 331780
  7.2 57.0 %copy-start.18 = (f32[2304]{0:T(1024)S(1)}, f32[2304]{0:T(1024)}, u32[]{:S(2)}) copy-start(f32[2304]{0:T(1024)} %param.24) | copy-start | bytes 27652
  7.2 63.8 %all-gather.3.cloned.1.call-start = ((), (), s32[]{:S(2)}) async-start(), calls=%async_computation.4 | async-start | bytes 5308416 | tf_op jit(solution)/shard_map/all_gather | solution.py:77
  7.9 76.1 %all-gather.5.cloned.1.call-start = ((), (), s32[]{:S(2)}) async-start(), calls=%async_computation.5 | async-start | bytes 1327104 | tf_op jit(solution)/shard_map/all_gather | solution.py:80
  8.7 176.3 %all-reduce.3.cloned.1.call-start = ((), (), s32[]{:S(2)}) async-start(), calls=%async_computation.6 | async-start | bytes 4718592 | tf_op jit(solution)/shard_map/psum | solution.py:157
  10.4 53.8 %copy-start.5 = (bf16[256,2304]{1,0:T(8,128)(2,1)S(1)}, bf16[256,2304]{1,0:T(8,128)(2,1)}, u32[]{:S(2)}) copy-start(bf16[256,2304]{1,0:T(8,128)(2,1)} %param.18) | copy-start | bytes 3538948
  71.0 1.5 copy-start.6
  71.0 2.5 slice-start
  73.6 1.8 copy-start.10
  78.1 3.4 copy-start.12
  93.1 97.8 %all-to-all-start.1 = ((bf16[8,1,72]{2,1,0:T(2,128)(2,1)}), bf16[8,1,72]{2,1,0:T(2,128)(2,1)S(1)}, u32[]{:S(2)}, u32[]{:S(2)}) async-start(bf16[8,1,72]{2,1,0:T(2,128)(2,1)} %all_to_all.20), calls=%async_computation.1 | async-start | bytes 8192 | tf_op jit(solution)/shard_map/all_to_all | solution.py:206
  96.6 90.9 %copy-start.17 = (f32[2304]{0:T(1024)S(1)}, f32[2304]{0:T(1024)}, u32[]{:S(2)}) copy-start(f32[2304]{0:T(1024)} %param.25) | copy-start | bytes 27652
  185.0 2.7 copy-start.2
  185.0 3.0 copy-start.7
  190.9 8.5 %all-to-all-start.2 = ((bf16[8,72,16]{1,2,0:T(8,128)(2,1)}), bf16[8,72,16]{1,2,0:T(8,128)(2,1)S(1)}, u32[]{:S(2)}, u32[]{:S(2)}) async-start(bf16[8,72,16]{1,2,0:T(8,128)(2,1)} %copy.92), calls=%async_computation.2 | async-start | bytes 65536 | tf_op jit(solution)/shard_map/all_to_all | solution.py:203
  199.4 36.2 %all-to-all-start = ((bf16[8,72,2304]{2,1,0:T(8,128)(2,1)}), bf16[8,72,2304]{2,1,0:T(8,128)(2,1)S(1)}, u32[]{:S(2)}, u32[]{:S(2)}) async-start(bf16[8,72,2304]{2,1,0:T(8,128)(2,1)} %bitcast.55), calls=%async_computation | async-start | bytes 5308416 | tf_op jit(solution)/shard_map/all_to_all | solution.py:200
  235.6 11.4 %copy-start.11 = (bf16[1,256,2,1440]{1,3,2,0:T(8,128)(2,1)S(1)}, bf16[1,256,2,1440]{1,3,2,0:T(8,128)(2,1)}, u32[]{:S(2)}) copy-start(bf16[1,256,2,1440]{1,3,2,0:T(8,128)(2,1)} %param.31) | copy-start | bytes 4423684
  257.5 5.1 %copy-start.4 = (bf16[256,2304]{1,0:T(8,128)(2,1)S(1)}, bf16[256,2304]{1,0:T(8,128)(2,1)}, u32[]{:S(2)}) copy-start(bf16[256,2304]{1,0:T(8,128)(2,1)} %copy-done.3) | copy-start | bytes 3538948
  257.5 5.1 %copy-start.15 = (bf16[2304,8]{0,1:T(8,128)(2,1)S(1)}, bf16[2304,8]{0,1:T(8,128)(2,1)}, u32[]{:S(2)}) copy-start(bf16[2304,8]{0,1:T(8,128)(2,1)} %param.28) | copy-start | bytes 110596
  257.5 37.1 %all-to-all-start.3 = ((bf16[8,72,2304]{2,1,0:T(8,128)(2,1)}), bf16[8,72,2304]{2,1,0:T(8,128)(2,1)}, u32[]{:S(2)}, u32[]{:S(2)}) async-start(bf16[8,72,2304]{2,1,0:T(8,128)(2,1)} %bitcast.152), calls=%async_computation.3 | async-start | bytes 5308416 | tf_op jit(solution)/shard_map/all_to_all | solution.py:233
  262.0 91.8 %all-reduce.5.cloned.1.call-start = ((), (), s32[]{:S(2)}) async-start(), calls=%async_computation.7 | async-start | bytes 2359296 | tf_op jit(solution)/shard_map/psum | solution.py:240
  294.6 7.0 %copy-start.13 = (bf16[256,9,32]{0,2,1:T(8,128)(2,1)S(1)}, bf16[256,9,32]{0,2,1:T(8,128)(2,1)}, u32[]{:S(2)}) copy-start(bf16[256,9,32]{0,2,1:T(8,128)(2,1)} %copy-done.12) | copy-start | bytes 442372
  305.5 52.0 %copy-start.1 = (bf16[576,2304]{1,0:T(8,128)(2,1)S(1)}, bf16[576,2304]{1,0:T(8,128)(2,1)}, u32[]{:S(2)}) copy-start(bf16[576,2304]{1,0:T(8,128)(2,1)} %param.27) | copy-start | bytes 7962628
  (5 other events, 5.6 us)
Sparse Core Ops, SparseCore 0:
  9.9 42.8 all-gather.2
  54.7 24.0 all-gather.4
  89.3 95.5 all-reduce.2
  300.6 53.1 all-reduce.4
where the time goes:
time: 365 us; the launch traced here: 364 us
  waiting for transfers between devices  192 us (53%)
  matrix products  52.9 us (14%)
  other arithmetic  35.5 us (10%)
  local copies, waits for them, and re-layouts  29.5 us (8%)
  blocking collectives  24 us (7%)
  starting transfers between devices  15.6 us (4%)
  between operations  14.2 us (4%)
    psum x1, waiting for transfers between devices, per_device(): mixed_out = lax.psum(head_term, 'tp')  88.4 us
    psum x1, waiting for transfers between devices, per_device(): moe_sum = lax.psum(moe_part.astype(jnp.bfloat16), 'tp').astype(jnp.float32)  41.7 us
    all_to_all x1, waiting for transfers between devices, per_device(): lax.all_to_all(spread_copies(send_rows), 'req', split_axis=0, concat_axis...  32.1 us
    all_to_all x1, waiting for transfers between devices, per_device(): lax.all_to_all(partial_term.reshape(n_req, count, D), 'req', split_axis=0...  27.5 us
    gather x3, other arithmetic, per_device(): token_slot = slot_of[adapter]  12.5 us
    unnamed x40, local copies, waits for them, and re-layouts  12.2 us
    all_gather x1, blocking collectives, per_device(): lax.all_gather(pool_aout, 'req', axis=0, tiled=True)  12 us
    all_gather x1, blocking collectives, per_device(): lax.all_gather(slot_query_key_value_up, 'req', axis=0, tiled=True)  12 us
  transfers between devices with their start and end apart: 8, of which 5 were waited for; matrix products, arithmetic and copies ran while one was open for 20% of the time, Pallas kernels for 0%

commit v1 on v0

v1 whole, which is shorter than its diff:
```python
import math

import jax
import jax.numpy as jnp
import numpy as np
from jax import lax
from jax.sharding import PartitionSpec as P

HEAD_SIZE = 64
EXPERTS = 8
ADAPTER_RANK = 16
PAGE = 128
CAP = 72
PIECES = 2

epsilon = 1e-05
adapter_scale = 2.0
rope_base = 10000.0

BF = jnp.bfloat16
F32 = jnp.float32


def iota(shape, dim):
    return lax.broadcasted_iota(jnp.int32, shape, dim)


def dot(a, b):
    return jnp.dot(a, b, preferred_element_type=F32)


def dot_nt(a, b):
    return lax.dot_general(a, b, (((1,), (1,)), ((), ())), preferred_element_type=F32)


def dot_tn(a, b):
    return lax.dot_general(a, b, (((0,), (0,)), ((), ())), preferred_element_type=F32)


def split_two(x):
    high = lax.reduce_precision(x, 8, 7)
    return high.astype(BF), (x - high).astype(BF)


def rope_tables(count):
    half = HEAD_SIZE // 2
    frequency = np.float32(rope_base) ** (-np.arange(half, dtype=np.float32) * np.float32(2.0) / HEAD_SIZE)
    angles = np.arange(count, dtype=np.float32)[:, None] * frequency[None, :].astype(np.float32)
    table = np.concatenate([np.cos(angles), np.sin(angles)], axis=1).astype(np.float32)
    parts = []
    for _ in range(3):
        part = table.astype(BF)
        parts.append(part)
        table = table - part.astype(np.float32)
    return np.concatenate(parts, axis=0)


def pieces_of(width):
    units = width // 128
    sizes = [(units * (i + 1)) // PIECES - (units * i) // PIECES for i in range(PIECES)]
    sizes[-1] += 0
    cuts, at = [], 0
    for i, size in enumerate(sizes):
        end = width if i == PIECES - 1 else at + size * 128
        cuts.append((at, end))
        at = end
    return cuts


def sum_tp(x, earlier):
    if earlier:
        x, _ = lax.optimization_barrier((x, earlier[-1]))
    return lax.psum(x, "tp")


def per_device(
    activations,
    lengths,
    adapter_of,
    slot_of,
    page_table,
    experts_of,
    attn_gain,
    moe_gain,
    w_qkv,
    output_weight,
    router,
    w_gate_up,
    w_down,
    expert_up_factors,
    pool_a,
    slot_query_key_value_up,
    pool_aout,
    pool_bout,
):
    T, D = activations.shape
    n_req = lax.axis_size("req")
    n_tp = lax.axis_size("tp")
    R = ADAPTER_RANK
    width = w_qkv.shape[2]
    heads = width // HEAD_SIZE
    own = pool_a.shape[0]
    n_slots = own * n_req
    n_adapters = slot_of.shape[0]
    share = D // n_tp
    pad = -share % 128
    pad_w = -width % 128

    my_tp = lax.axis_index("tp")
    down_t = pool_a.transpose(0, 2, 1)
    down_part = lax.dynamic_slice_in_dim(down_t[:, : 3 * R], my_tp * share, share, 2)
    up_t = slot_query_key_value_up.transpose(0, 2, 1, 3).reshape(own, 3 * R, width)
    aout_t = pool_aout.transpose(0, 2, 1)
    pool_down = lax.all_gather(
        jnp.pad(down_part, ((0, 0), (0, 0), (0, pad))), "req", axis=0, tiled=True
    )[:, :, :share]
    pool_up = lax.all_gather(
        jnp.pad(jnp.concatenate([up_t, aout_t], axis=1), ((0, 0), (0, 0), (0, pad_w))),
        "req",
        axis=0,
        tiled=True,
    )[:, :, :width]
    pool_exp = lax.all_gather(down_t[:, 3 * R :], "req", axis=0, tiled=True)
    pool_bup = lax.all_gather(pool_bout, "req", axis=0, tiled=True)

    row = lengths[0]
    n_in = row.shape[0]
    ends = jnp.sum(jnp.where(iota((n_in, n_in), 0) <= iota((n_in, n_in), 1), row[:, None], 0), axis=0)
    starts = ends - row
    pages = (row + PAGE - 1) // PAGE
    first_page = jnp.sum(
        jnp.where(iota((n_in, n_in), 0) < iota((n_in, n_in), 1), pages[:, None], 0), axis=0
    )
    slots_in = jnp.sum(
        jnp.where(
            adapter_of[0][:, None] == iota((n_in, n_adapters), 1), slot_of[None, :], 0
        ),
        axis=1,
    )
    place = iota((T, n_in), 0)
    here = (place >= starts[None, :]) & (place < ends[None, :])

    def of_request(values):
        return jnp.sum(jnp.where(here, values[None, :], 0), axis=1, keepdims=True)

    start = of_request(starts)
    token_slot = of_request(slots_in)
    adapter = of_request(adapter_of[0])
    position = iota((T, 1), 0) - start
    page_at = of_request(first_page) + position // PAGE
    n_pages = page_table.shape[1]
    local_page = jnp.sum(
        jnp.where(page_at == iota((T, n_pages), 1), page_table, 0), axis=1, keepdims=True
    )
    cache_row = local_page * PAGE + position % PAGE

    def slot_mask(each):
        return token_slot == iota((T, n_slots * each), 1) // each

    mask_r = slot_mask(R)

    act = activations.astype(F32)
    mean_sq = jnp.mean(act * act, axis=-1, keepdims=True)
    normed = (act * lax.rsqrt(mean_sq + epsilon) * attn_gain).astype(BF)
    normed = lax.optimization_barrier(normed)
    plain = [dot_nt(w_qkv[:, p].T, normed) for p in range(3)]
    normed_part = lax.dynamic_slice_in_dim(normed, my_tp * share, share, 1)
    coeff_mask = slot_mask(1)
    down_all = dot_nt(
        pool_down.transpose(1, 0, 2).reshape(3 * R * n_slots, share), normed_part
    ).reshape(3 * R, n_slots, T)
    slot_row = coeff_mask.T
    coeff_part = jnp.sum(jnp.where(slot_row[None], down_all, 0.0), axis=1)
    coeff = lax.psum(coeff_part, "tp").astype(BF)

    projected = []
    for p in range(3):
        spread = jnp.where(
            slot_row[:, None, :],
            coeff[p * R : (p + 1) * R][None] * jnp.array(adapter_scale, BF),
            jnp.zeros((), BF),
        ).reshape(n_slots * R, T)
        up = pool_up[:, p * R : (p + 1) * R].reshape(n_slots * R, width)
        projected.append(plain[p] + dot_tn(up, spread))

    tables = jnp.asarray(rope_tables(T))
    hot = (position == iota((T, T), 1)).astype(BF)
    turned = lax.dot_general(
        tables,
        jnp.concatenate([hot, hot, hot], axis=1),
        (((0,), (1,)), ((), ())),
        preferred_element_type=F32,
    )
    half = HEAD_SIZE // 2
    cosine, sine = turned[None, :half], turned[None, half:]

    def rotate(x):
        x = x.reshape(heads, HEAD_SIZE, T)
        front, back = x[:, :half], x[:, half:]
        return jnp.concatenate(
            [front * cosine - back * sine, back * cosine + front * sine], axis=1
        ).astype(BF)

    queries = rotate(projected[0])
    keys = rotate(projected[1])
    values = projected[2].astype(BF).reshape(heads, HEAD_SIZE, T)

    place_hot = (cache_row == iota((T, n_pages * PAGE), 1)).astype(BF)
    cache = [
        lax.dot_general(
            place_hot, x.reshape(width, T), (((0,), (1,)), ((), ())), preferred_element_type=F32
        )
        .astype(BF)
        .reshape(n_pages, PAGE, width)
        for x in (keys, values)
    ]
    page_cache = jnp.stack(cache, axis=2)

    scores = jnp.einsum("hdq,hdk->hqk", queries, keys, preferred_element_type=F32) * (
        1.0 / math.sqrt(HEAD_SIZE)
    )
    seen = iota((T, T), 1)
    allowed = (seen <= iota((T, T), 0)) & (seen >= start)
    scores = jnp.where(allowed[None], scores, -1e30)
    weights = jnp.exp(scores - jnp.max(scores, axis=-1, keepdims=True))
    weights = (weights / jnp.sum(weights, axis=-1, keepdims=True)).astype(BF)
    attended = (
        jnp.einsum("hqk,hdk->qhd", weights, values, preferred_element_type=F32)
        .astype(BF)
        .reshape(T, width)
    )

    aout_all = dot_nt(attended, pool_up[:, 3 * R :].reshape(n_slots * R, width))
    spread_hi, spread_lo = split_two(jnp.where(mask_r, adapter_scale * aout_all, 0.0))
    cuts = pieces_of(D)
    bup = pool_bup.reshape(n_slots * R, D)
    mixed = []
    for at, end in cuts:
        term = (
            dot(attended, output_weight[:, at:end])
            + dot(spread_hi, bup[:, at:end])
            + dot(spread_lo, bup[:, at:end])
        )
        mixed.append(sum_tp(term.astype(BF), mixed))

    split = n_req // EXPERTS
    experts = [experts_of[:, k : k + 1] for k in range(2)]
    hots = [e == iota((T, EXPERTS), 1) for e in experts]
    chosen_any = (hots[0] | hots[1]).astype(BF)
    before = (iota((T, T), 1) < iota((T, T), 0)).astype(BF)
    prior = dot(before, chosen_any).astype(jnp.int32)
    picks = []
    for k in range(2):
        order = jnp.sum(jnp.where(hots[k], prior, 0), axis=1, keepdims=True)
        picks.append(experts[k] * CAP + order == iota((T, EXPERTS * CAP), 1))
    route = (picks[0] | picks[1]).astype(BF)

    def send(x):
        rows = dot_tn(route, x).astype(BF).reshape(EXPERTS, 1, CAP, x.shape[1])
        rows = jnp.broadcast_to(rows, (EXPERTS, split, CAP, x.shape[1]))
        got = lax.all_to_all(
            rows.reshape(n_req, CAP, x.shape[1]), "req", split_axis=0, concat_axis=0, tiled=True
        )
        return got.reshape(n_req * CAP, x.shape[1])

    units = w_gate_up.shape[3]
    residual = []
    pre = []
    before_act = None
    square = 0.0
    for (at, end), mix in zip(cuts, mixed):
        res = act[:, at:end] + mix.astype(F32)
        residual.append(res)
        square = square + jnp.sum(res * res, axis=-1, keepdims=True)
        pre_p = (res * moe_gain[None, at:end]).astype(BF)
        pre.append(pre_p)
        rows = send(pre_p)
        gu = w_gate_up[0, at:end].reshape(end - at, 2 * units)
        part = dot(rows, gu)
        before_act = part if before_act is None else before_act + part
    scale = lax.rsqrt(square / D + epsilon)
    exp_all = 0.0
    logits = 0.0
    pool_exp = pool_exp.reshape(n_slots * R, D)
    for (at, end), pre_p in zip(cuts, pre):
        exp_all = exp_all + dot_nt(pre_p, pool_exp[:, at:end])
        logits = logits + dot(pre_p, router[at:end])
    logits = logits * scale
    coeff_exp = jnp.where(mask_r, exp_all * scale, 0.0).astype(BF)
    fold = (iota((n_slots * R, R), 0) % R == iota((n_slots * R, R), 1)).astype(BF)
    coeff_exp = dot(coeff_exp, fold).astype(BF)
    scale_hi, scale_lo = split_two(scale)
    meta = jnp.concatenate([coeff_exp, adapter.astype(BF), scale_hi, scale_lo], axis=1)
    got = send(meta)
    got_coeff = got[:, :R]
    got_ids = got[:, R : R + 1].astype(jnp.int32)
    got_scale = got[:, R + 1 : R + 2].astype(F32) + got[:, R + 2 : R + 3].astype(F32)
    unfold = (iota((R, n_adapters * R), 1) % R == iota((R, n_adapters * R), 0)).astype(BF)
    broad = dot(got_coeff * jnp.array(adapter_scale, BF), unfold)
    broad = jnp.where(
        got_ids == iota((n_req * CAP, n_adapters * R), 1) // R, broad, 0.0
    ).astype(BF)
    before_act = before_act * got_scale + dot(
        broad, expert_up_factors[0].reshape(n_adapters * R, 2 * units)
    )
    hidden = (jax.nn.silu(before_act[:, :units]) * before_act[:, units:]).astype(BF)

    chosen = [
        jnp.sum(jnp.where(hots[k], logits, 0.0), axis=1, keepdims=True) for k in range(2)
    ]
    gates = [1.0 / (1.0 + jnp.exp(chosen[1 - k] - chosen[k])) for k in range(2)]
    combine = jnp.where(picks[0], gates[0], 0.0) + jnp.where(picks[1], gates[1], 0.0)
    combine = jnp.broadcast_to(
        combine.reshape(T, EXPERTS, 1, CAP), (T, EXPERTS, split, CAP)
    ).reshape(T, n_req * CAP)
    combine_hi, combine_lo = split_two(combine)

    outs, moe_sums = [], []
    for (at, end), res in zip(cuts, residual):
        part = dot(hidden, w_down[0][:, at:end]).astype(BF)
        back = lax.all_to_all(
            part.reshape(n_req, CAP, end - at), "req", split_axis=0, concat_axis=0, tiled=True
        ).reshape(n_req * CAP, end - at)
        moe = dot(combine_hi, back) + dot(combine_lo, back)
        moe_sums.append(sum_tp(moe.astype(BF), moe_sums))
        outs.append((res + moe_sums[-1].astype(F32)).astype(BF))
    layer_out = jnp.concatenate(outs, axis=1)
    return (layer_out, page_cache)


def solution(mesh):
    return jax.shard_map(
        per_device,
        mesh=mesh,
        in_specs=(
            P("req", None),
            P("req", None),
            P("req", None),
            P(),
            P("req", None),
            P("req", None),
            P(),
            P(),
            P(None, None, "tp"),
            P("tp", None),
            P(),
            P("req", None, None, "tp"),
            P("req", "tp", None),
            P("req", None, None, "tp"),
            P("req", None, None),
            P("req", None, None, "tp"),
            P("req", "tp", None),
            P("req", None, None),
        ),
        out_specs=(P("req", None), P("req", None, None, "tp")),
        check_vma=False,
    )
```

time: 365 us -> 402 us (1.10)
  matrix products: 52.9 us -> 91.2 us
  other arithmetic: 35.5 us -> 22.2 us
  blocking collectives: 24 us -> 33.6 us
  local copies, waits for them, and re-layouts: 29.5 us -> 23.7 us
  starting transfers between devices: 15.6 us -> 21.4 us
    dot_general x14 -> x37, matrix products: 47.5 us -> 87.8 us  [the longest x19 65.6 us: dot(): return jnp.dot(a, b, preferred_element_type=F32)]
    all_gather x2 -> x3, waiting for transfers between devices: 0.02 us -> 23.8 us  [the longest x1 23.8 us: per_device(): pool_exp = lax.all_gather(down_t[:, 3 * R:], 'req', axis=0, tiled=True)]
    all_to_all x4 -> x5, waiting for transfers between devices: 60.8 us -> 40.7 us  [the longest x2 24.5 us: per_device(): lax.all_to_all(part.reshape(n_req, CAP, end - at), 'req', split_axis=0, c...]
    psum x0 -> x1, blocking collectives: none -> 19.3 us  [per_device(): coeff = lax.psum(coeff_part, 'tp').astype(BF)]
    gather x4 -> x0, other arithmetic: 12.5 us -> none  [the longest x3 12.5 us: per_device(): token_slot = slot_of[adapter]]
    slice x6 -> x7, local copies, waits for them, and re-layouts: 2.4 us -> 12.1 us  [the longest x1 10.6 us: per_device(): gu = w_gate_up[0, at:end].reshape(end - at, 2 * units)]
    gather x9 -> x0, local copies, waits for them, and re-layouts: 9.67 us -> none  [the longest x5 4.05 us: per_device(): chosen = jnp.take_along_axis(logits, experts_of, axis=1)]
    all_gather x2 -> x1, blocking collectives: 24 us -> 14.3 us  [per_device(): lax.all_gather(jnp.pad(down_part, ((0, 0), (0, 0), (0, pad))), 'req', axi...]
  transfers between devices with their start and end apart: 8 -> 12, of which waited for: 5 -> 10; matrix products, arithmetic and copies ran while one was open for 20% -> 23% of each run, Pallas kernels for 0% -> 0%
where the time goes in v1:
time: 402 us; the launch traced here: 400 us
  waiting for transfers between devices  194 us (48%)
  matrix products  91.2 us (23%)
  blocking collectives  33.6 us (8%)
  local copies, waits for them, and re-layouts  23.7 us (6%)
  other arithmetic  22.2 us (6%)
  starting transfers between devices  21.4 us (5%)
  between operations  14.7 us (4%)
    psum x4, waiting for transfers between devices, sum_tp(): return lax.psum(x, 'tp')  128 us
    dot_general x19, matrix products, dot(): return jnp.dot(a, b, preferred_element_type=F32)  65.6 us
    all_to_all x2, waiting for transfers between devices, per_device(): lax.all_to_all(part.reshape(n_req, CAP, end - at), 'req', split_axis=0, c...  24.5 us
    all_gather x1, waiting for transfers between devices, per_device(): pool_exp = lax.all_gather(down_t[:, 3 * R:], 'req', axis=0, tiled=True)  23.8 us
    psum x1, blocking collectives, per_device(): coeff = lax.psum(coeff_part, 'tp').astype(BF)  19.3 us
    all_to_all x3, waiting for transfers between devices, send(): lax.all_to_all(rows.reshape(n_req, CAP, x.shape[1]), 'req', split_axis=0,...  16.2 us
    all_gather x1, blocking collectives, per_device(): lax.all_gather(jnp.pad(down_part, ((0, 0), (0, 0), (0, pad))), 'req', axi...  14.3 us
    all_to_all x3, starting transfers between devices, send(): lax.all_to_all(rows.reshape(n_req, CAP, x.shape[1]), 'req', split_axis=0,...  11.9 us
  transfers between devices with their start and end apart: 12, of which 10 were waited for; matrix products, arithmetic and copies ran while one was open for 23% of the time, Pallas kernels for 0%

profile of v1, /device:TPU:0, one launch (start us, length us, event | category | flops | bytes accessed | tf_op | source)
XLA Modules:
  0.0 400.5 jit_solution(13549057890292628473)
XLA Ops:
  18.5 14.3 %all_gather.13 = bf16[16,48,640]{2,1,0:T(8,128)(2,1)} all-gather(bf16[2,48,640]{2,1,0:T(8,128)(2,1)S(1)} %pad.9), channel_id=1, replica_groups=mesh['req'=8,'tp'=4] {'req'}, dimensions={0}, use_global_device_ids=true | all-gather | bytes 1105920 | tf_op jit(solution)/shard_map/all_gather | solution.py:114
  36.6 19.3 %psum.35 = bf16[48,256]{1,0:T(8,128)(2,1)S(1)} all-reduce(f32[48,256]{1,0:T(8,128)S(1)} %fusion.52), channel_id=1, replica_groups=mesh['req'=8,'tp'=4] {'tp'}, use_global_device_ids=true, to_apply=%region_5.6 | all-reduce | flops 12288 | bytes 73728 | tf_op jit(solution)/shard_map/psum | solution.py:174
  66.4 3.4 fusion.196
  84.8 33.7 %all-reduce.7.cloned.1.call-done = bf16[256,1152]{0,1:T(8,128)(2,1)} async-done(((bf16[256,1152]{0,1:T(8,128)(2,1)}), bf16[256,1152]{0,1:T(8,128)(2,1)}) %all-reduce.7.cloned.1.call-update) | async-done | bytes 589840 | tf_op jit(solution)/shard_map/psum | solution.py:73
  121.4 38.7 %all-reduce.9.cloned.1.call-done = bf16[256,1152]{0,1:T(8,128)(2,1)} async-done(((bf16[256,1152]{0,1:T(8,128)(2,1)}), bf16[256,1152]{0,1:T(8,128)(2,1)}) %all-reduce.9.cloned.1.call-update) | async-done | bytes 589840 | tf_op jit(solution)/shard_map/psum | solution.py:73
  162.4 23.8 %all-gather.8.cloned.1.call-done = bf16[16,16,2304]{2,1,0:T(8,128)(2,1)} async-done(((bf16[2,16,2304]{2,1,0:T(8,128)(2,1)}), bf16[16,16,2304]{2,1,0:T(8,128)(2,1)}) %all-gather.8.cloned.1.call-update) | async-done | bytes 1179664 | tf_op jit(solution)/shard_map/all_gather | solution.py:123
  190.5 3.3 all-to-all-start.2
  198.5 4.3 %all-to-all-start.1 = ((bf16[8,72,1152]{2,1,0:T(8,128)(2,1)}), bf16[8,72,1152]{2,1,0:T(8,128)(2,1)}, u32[]{:S(2)}, u32[]{:S(2)}) async-start(bf16[8,72,1152]{2,1,0:T(8,128)(2,1)} %bitcast.37), calls=%async_computation.1 | async-start | bytes 2654208 | tf_op jit(solution)/shard_map/all_to_all | solution.py:261
  202.8 10.6 %fusion.192 = (bf16[1,1152,2,1440]{1,3,2,0:T(8,128)(2,1)}, bf16[1,1152,2,1440]{1,3,2,0:T(8,128)(2,1)}) fusion(bf16[1,2304,2,1440]{1,3,2,0:T(8,128)(2,1)} %param.30), kind=kLoop, calls=%fused_computation.272 | loop fusion | bytes 26542080 | tf_op jit(solution)/shard_map/slice | solution.py:278
  215.5 5.7 %all-to-all-done.1 = bf16[8,72,1152]{2,1,0:T(8,128)(2,1)} async-done(((bf16[8,72,1152]{2,1,0:T(8,128)(2,1)}), bf16[8,72,1152]{2,1,0:T(8,128)(2,1)}, u32[]{:S(2)}, u32[]{:S(2)}) %all-to-all-start.1) | async-done | bytes 1327136 | tf_op jit(solution)/shard_map/all_to_all | solution.py:261
  221.2 4.3 %all-to-all-start = ((bf16[8,72,1152]{2,1,0:T(8,128)(2,1)}), bf16[8,72,1152]{2,1,0:T(8,128)(2,1)}, u32[]{:S(2)}, u32[]{:S(2)}) async-start(bf16[8,72,1152]{2,1,0:T(8,128)(2,1)} %bitcast.34), calls=%async_computation | async-start | bytes 2654208 | tf_op jit(solution)/shard_map/all_to_all | solution.py:261
  225.6 10.8 %fusion.200 = f32[576,2880]{1,0:T(8,128)} fusion(bf16[576,1152]{1,0:T(8,128)(2,1)} %bitcast.38, bf16[1152,2880]{0,1:T(8,128)(2,1)} %bitcast.138), kind=kOutput, calls=%fused_computation.279 | convolution fusion | flops 3822059520 | bytes 14598144 | tf_op jit(solution)/shard_map/dot_general | solution.py:29
  236.4 7.5 %all-to-all-done = bf16[8,72,1152]{2,1,0:T(8,128)(2,1)} async-done(((bf16[8,72,1152]{2,1,0:T(8,128)(2,1)}), bf16[8,72,1152]{2,1,0:T(8,128)(2,1)}, u32[]{:S(2)}, u32[]{:S(2)}) %all-to-all-start) | async-done | bytes 1327136 | tf_op jit(solution)/shard_map/all_to_all | solution.py:261
  243.9 10.9 %fusion.199 = f32[576,2880]{1,0:T(8,128)} fusion(bf16[576,1152]{1,0:T(8,128)(2,1)} %bitcast.35, bf16[1152,2880]{0,1:T(8,128)(2,1)} %bitcast.137), kind=kOutput, calls=%fused_computation.278 | convolution fusion | flops 3822059520 | bytes 14598144 | tf_op jit(solution)/shard_map/dot_general | solution.py:29
  254.8 9.0 %multiply_add_fusion = f32[576,2880]{1,0:T(8,128)} fusion(f32[576,2880]{1,0:T(8,128)} %fusion.199, f32[576,2880]{1,0:T(8,128)} %fusion.200, bf16[256,2880]{0,1:T(8,128)(2,1)S(1)} %bitcast.136, f32[576]{0:T(1024)S(1)} %fusion.165, s32[256]{0:T(256)S(1)} %get-tuple-element.57, s32[256]{0:T(256)S(1)} %get-tuple-element.58, s32[576]{0:T(1024)S(1)} %fusion.163, ...), kind=kOutput, calls=%fused_computation.1 | convolution fusion | flops 859649024 | bytes 21414912 | tf_op jit(solution)/shard_map/dot_general | solution.py:29
  263.8 4.4 %fusion.1 = bf16[576,1440]{1,0:T(8,128)(2,1)S(1)} fusion(f32[576,2880]{1,0:T(8,128)} %multiply_add_fusion), kind=kLoop, calls=%fused_computation.3 | loop fusion | flops 4976640 | bytes 8294400 | tf_op jit(solution)/shard_map/convert_element_type | solution.py:306
  268.2 6.2 %fusion.6 = bf16[576,1152]{1,0:T(8,128)(2,1)} fusion(bf16[576,1440]{1,0:T(8,128)(2,1)S(1)} %fusion.1, bf16[1440,2304]{1,0:T(8,128)(2,1)} %bitcast.187), kind=kOutput, calls=%fused_computation.8 | convolution fusion | flops 1911693312 | bytes 6303744 | tf_op jit(solution)/shard_map/dot_general | solution.py:29
  274.4 4.6 %all-to-all-start.3 = ((bf16[8,72,1152]{2,1,0:T(8,128)(2,1)}), bf16[8,72,1152]{2,1,0:T(8,128)(2,1)}, u32[]{:S(2)}, u32[]{:S(2)}) async-start(bf16[8,72,1152]{2,1,0:T(8,128)(2,1)} %bitcast.146), calls=%async_computation.3 | async-start | bytes 2654208 | tf_op jit(solution)/shard_map/all_to_all | solution.py:321
  279.1 6.0 %fusion.9 = bf16[576,1152]{1,0:T(8,128)(2,1)} fusion(bf16[576,1440]{1,0:T(8,128)(2,1)} %copy-done.5, bf16[1440,2304]{1,0:T(8,128)(2,1)} %bitcast.188), kind=kOutput, calls=%fused_computation.9 | convolution fusion | flops 1911693312 | bytes 6414336 | tf_op jit(solution)/shard_map/dot_general | solution.py:29
  285.1 12.1 %all-to-all-done.3 = bf16[8,72,1152]{2,1,0:T(8,128)(2,1)} async-done(((bf16[8,72,1152]{2,1,0:T(8,128)(2,1)}), bf16[8,72,1152]{2,1,0:T(8,128)(2,1)}, u32[]{:S(2)}, u32[]{:S(2)}) %all-to-all-start.3) | async-done | bytes 1327136 | tf_op jit(solution)/shard_map/all_to_all | solution.py:321
  297.2 4.4 %all-to-all-start.4 = ((bf16[8,72,1152]{2,1,0:T(8,128)(2,1)}), bf16[8,72,1152]{2,1,0:T(8,128)(2,1)}, u32[]{:S(2)}, u32[]{:S(2)}) async-start(bf16[8,72,1152]{2,1,0:T(8,128)(2,1)} %bitcast.145), calls=%async_computation.4 | async-start | bytes 2654208 | tf_op jit(solution)/shard_map/all_to_all | solution.py:321
  307.6 12.4 %all-to-all-done.4 = bf16[8,72,1152]{2,1,0:T(8,128)(2,1)} async-done(((bf16[8,72,1152]{2,1,0:T(8,128)(2,1)}), bf16[8,72,1152]{2,1,0:T(8,128)(2,1)}, u32[]{:S(2)}, u32[]{:S(2)}) %all-to-all-start.4) | async-done | bytes 1327136 | tf_op jit(solution)/shard_map/all_to_all | solution.py:321
  325.5 22.7 %all-reduce.11.cloned.1.call-done = bf16[256,1152]{0,1:T(8,128)(2,1)} async-done(((bf16[256,1152]{0,1:T(8,128)(2,1)}), bf16[256,1152]{0,1:T(8,128)(2,1)}) %all-reduce.11.cloned.1.call-update) | async-done | bytes 589840 | tf_op jit(solution)/shard_map/psum | solution.py:73
  356.0 33.4 %all-reduce.13.cloned.1.call-done = bf16[256,1152]{0,1:T(8,128)(2,1)} async-done(((bf16[256,1152]{0,1:T(8,128)(2,1)}), bf16[256,1152]{0,1:T(8,128)(2,1)}) %all-reduce.13.cloned.1.call-update) | async-done | bytes 589840 | tf_op jit(solution)/shard_map/psum | solution.py:73
  (149 shorter events, 80.0 us)
Async XLA Ops:
  7.2 247.6 %copy-start = (bf16[1,256,2,1440]{1,3,2,0:T(8,128)(2,1)S(1)}, bf16[1,256,2,1440]{1,3,2,0:T(8,128)(2,1)}, u32[]{:S(2)}) copy-start(bf16[1,256,2,1440]{1,3,2,0:T(8,128)(2,1)} %param.32) | copy-start | bytes 4423684
  7.2 11.1 %copy-start.9 = (bf16[2,2304,64]{1,2,0:T(8,128)(2,1)S(1)}, bf16[2,2304,64]{1,2,0:T(8,128)(2,1)}, u32[]{:S(2)}) copy-start(bf16[2,2304,64]{1,2,0:T(8,128)(2,1)} %param.33) | copy-start | bytes 1769476
  7.2 48.8 %all-gather.4.cloned.1.call-start = ((), (), s32[]{:S(2)}) async-start(), calls=%async_computation.5 | async-start | bytes 1474560 | tf_op jit(solution)/shard_map/all_gather | solution.py:117
  9.0 69.5 %all-gather.6.cloned.1.call-start = ((), (), s32[]{:S(2)}) async-start(), calls=%async_computation.6 | async-start | bytes 1327104 | tf_op jit(solution)/shard_map/all_gather | solution.py:124
  9.8 108.7 %all-reduce.7.cloned.1.call-start = ((), (), s32[]{:S(2)}) async-start(), calls=%async_computation.7 | async-start | bytes 1179648 | tf_op jit(solution)/shard_map/psum | solution.py:73
  32.8 1.9 copy-start.20
  57.4 2.7 copy-start.16
  63.8 2.7 copy-start.10
  69.8 3.2 copy-start.22
  73.1 1.9 copy-start.3
  81.7 78.4 %all-reduce.9.cloned.1.call-start = ((), (), s32[]{:S(2)}) async-start(), calls=%async_computation.8 | async-start | bytes 1179648 | tf_op jit(solution)/shard_map/psum | solution.py:73
  118.5 67.6 %all-gather.8.cloned.1.call-start = ((), (), s32[]{:S(2)}) async-start(), calls=%async_computation.9 | async-start | bytes 1327104 | tf_op jit(solution)/shard_map/all_gather | solution.py:123
  119.5 40.6 %copy-start.4 = (bf16[256,1152]{0,1:T(8,128)(2,1)S(1)}, bf16[256,1152]{0,1:T(8,128)(2,1)}, u32[]{:S(2)}) copy-start(bf16[256,1152]{0,1:T(8,128)(2,1)} %all-reduce.7.cloned.1.call-done) | copy-start | bytes 1769476
  190.5 8.1 %all-to-all-start.2 = ((bf16[8,2,684]{2,1,0:T(2,128)(2,1)}), bf16[8,2,684]{2,1,0:T(2,128)(2,1)S(1)}, u32[]{:S(2)}, u32[]{:S(2)}) async-start(bf16[8,2,684]{2,1,0:T(2,128)(2,1)} %reshape.383), calls=%async_computation.2 | async-start | bytes 49152 | tf_op jit(solution)/shard_map/all_to_all | solution.py:261
  198.5 22.7 %all-to-all-start.1 = ((bf16[8,72,1152]{2,1,0:T(8,128)(2,1)}), bf16[8,72,1152]{2,1,0:T(8,128)(2,1)}, u32[]{:S(2)}, u32[]{:S(2)}) async-start(bf16[8,72,1152]{2,1,0:T(8,128)(2,1)} %bitcast.37), calls=%async_computation.1 | async-start | bytes 2654208 | tf_op jit(solution)/shard_map/all_to_all | solution.py:261
  221.2 22.7 %all-to-all-start = ((bf16[8,72,1152]{2,1,0:T(8,128)(2,1)}), bf16[8,72,1152]{2,1,0:T(8,128)(2,1)}, u32[]{:S(2)}, u32[]{:S(2)}) async-start(bf16[8,72,1152]{2,1,0:T(8,128)(2,1)} %bitcast.34), calls=%async_computation | async-start | bytes 2654208 | tf_op jit(solution)/shard_map/all_to_all | solution.py:261
  268.2 6.2 %copy-start.5 = (bf16[576,1440]{1,0:T(8,128)(2,1)}, bf16[576,1440]{1,0:T(8,128)(2,1)S(1)}, u32[]{:S(2)}) copy-start(bf16[576,1440]{1,0:T(8,128)(2,1)S(1)} %fusion.1) | copy-start | bytes 4976644
  274.4 4.6 %copy-start.11 = (bf16[9,32,256]{2,1,0:T(8,128)(2,1)S(1)}, bf16[9,32,256]{2,1,0:T(8,128)(2,1)}, u32[]{:S(2)}) copy-start(bf16[9,32,256]{2,1,0:T(8,128)(2,1)} %copy-done.10) | copy-start | bytes 442372
  274.4 4.6 %copy-start.12 = (bf16[9,32,256]{2,1,0:T(8,128)(2,1)S(1)}, bf16[9,32,256]{2,1,0:T(8,128)(2,1)}, u32[]{:S(2)}) copy-start(bf16[9,32,256]{2,1,0:T(8,128)(2,1)} %get-tuple-element.35) | copy-start | bytes 442372
  274.4 22.8 %all-to-all-start.3 = ((bf16[8,72,1152]{2,1,0:T(8,128)(2,1)}), bf16[8,72,1152]{2,1,0:T(8,128)(2,1)}, u32[]{:S(2)}, u32[]{:S(2)}) async-start(bf16[8,72,1152]{2,1,0:T(8,128)(2,1)} %bitcast.146), calls=%async_computation.3 | async-start | bytes 2654208 | tf_op jit(solution)/shard_map/all_to_all | solution.py:321
  297.2 4.5 %copy-start.18 = (bf16[2304,8]{0,1:T(8,128)(2,1)S(1)}, bf16[2304,8]{0,1:T(8,128)(2,1)}, u32[]{:S(2)}) copy-start(bf16[2304,8]{0,1:T(8,128)(2,1)} %param.29) | copy-start | bytes 110596
  297.2 22.8 %all-to-all-start.4 = ((bf16[8,72,1152]{2,1,0:T(8,128)(2,1)}), bf16[8,72,1152]{2,1,0:T(8,128)(2,1)}, u32[]{:S(2)}, u32[]{:S(2)}) async-start(bf16[8,72,1152]{2,1,0:T(8,128)(2,1)} %bitcast.145), calls=%async_computation.4 | async-start | bytes 2654208 | tf_op jit(solution)/shard_map/all_to_all | solution.py:321
  301.6 46.5 %all-reduce.11.cloned.1.call-start = ((), (), s32[]{:S(2)}) async-start(), calls=%async_computation.10 | async-start | bytes 1179648 | tf_op jit(solution)/shard_map/psum | solution.py:73
  307.6 81.7 %all-reduce.13.cloned.1.call-start = ((), (), s32[]{:S(2)}) async-start(), calls=%async_computation.11 | async-start | bytes 1179648 | tf_op jit(solution)/shard_map/psum | solution.py:73
  (11 other events, 16.1 us)
Sparse Core Ops, SparseCore 0:
  10.5 27.8 all-gather.3
  40.2 24.0 all-gather.5
  81.8 36.6 all-reduce.6
  121.3 38.7 all-reduce.8
  162.4 23.7 all-gather.7
  307.7 40.3 all-reduce.10
  350.5 38.7 all-reduce.12

commit v2 on v1

--- a/solution.py
+++ b/solution.py
@@ -1,9 +1,12 @@
+import functools
 import math
 
 import jax
 import jax.numpy as jnp
 import numpy as np
 from jax import lax
+from jax.experimental import pallas as pl
+from jax.experimental.pallas import tpu as pltpu
 from jax.sharding import PartitionSpec as P
 
 HEAD_SIZE = 64
@@ -11,7 +14,9 @@
 ADAPTER_RANK = 16
 PAGE = 128
 CAP = 72
-PIECES = 2
+PIECES = 3
+MESH = pl.DeviceIdType.MESH
+VMEM_BYTES = 44 * 2**20
 
 epsilon = 1e-05
 adapter_scale = 2.0
@@ -67,10 +72,255 @@
     return cuts
 
 
-def sum_tp(x, earlier):
-    if earlier:
-        x, _ = lax.optimization_barrier((x, earlier[-1]))
-    return lax.psum(x, "tp")
+def greet(tp_too, req_too, n_tp, n_req):
+    barrier = pltpu.get_barrier_semaphore()
+    count = 0
+    for axis, n, wanted in (("tp", n_tp, tp_too), ("req", n_req, req_too)):
+        if wanted:
+            me = lax.axis_index(axis)
+            for k in range(1, n):
+                pl.semaphore_signal(
+                    barrier, inc=1, device_id={axis: lax.rem(me + k, n)}, device_id_type=MESH
+                )
+            count += n - 1
+    pl.semaphore_wait(barrier, count)
+
+
+def remote(src, dst, send_sem, recv_sem, axis, peer):
+    return pltpu.make_async_remote_copy(
+        src_ref=src,
+        dst_ref=dst,
+        send_sem=send_sem,
+        recv_sem=recv_sem,
+        device_id={axis: peer},
+        device_id_type=MESH,
+    )
+
+
+def small_sum_kernel(n_tp, x_ref, o_ref, buf, send, recv):
+    me = lax.axis_index("tp")
+    greet(True, False, n_tp, 1)
+    copies = []
+    for k in range(1, n_tp):
+        c = remote(x_ref, buf.at[k - 1], send.at[k], recv.at[k], "tp", lax.rem(me + k, n_tp))
+        c.start()
+        copies.append(c)
+    total = x_ref[...]
+    for c in copies:
+        c.wait_recv()
+    for k in range(1, n_tp):
+        total = total + buf[k - 1]
+    o_ref[...] = total
+    for c in copies:
+        c.wait_send()
+
+
+def small_sum(x, n_tp):
+    return pl.pallas_call(
+        functools.partial(small_sum_kernel, n_tp),
+        out_shape=jax.ShapeDtypeStruct(x.shape, x.dtype),
+        in_specs=[pl.BlockSpec(memory_space=pltpu.VMEM)],
+        out_specs=pl.BlockSpec(memory_space=pltpu.VMEM),
+        scratch_shapes=[
+            pltpu.VMEM((n_tp - 1,) + x.shape, x.dtype),
+            pltpu.SemaphoreType.DMA((n_tp,)),
+            pltpu.SemaphoreType.DMA((n_tp,)),
+        ],
+        compiler_params=pltpu.CompilerParams(
+            collective_id=0, has_side_effects=True, vmem_limit_bytes=VMEM_BYTES
+        ),
+    )(x)
+
+
+def dispatch_kernel(
+    n_tp, n_req, term, act, gain, route, rows, normed, res, rs_buf, out_buf,
+    rs_send, rs_recv, ag_send, ag_recv, a2a_send, a2a_recv,
+):
+    my, me = lax.axis_index("tp"), lax.axis_index("req")
+    chunk, D = act.shape
+    split = n_req // EXPERTS
+    greet(True, True, n_tp, n_req)
+    copies = []
+    for k in range(1, n_tp):
+        peer = lax.rem(my + k, n_tp)
+        c = remote(term.at[peer], rs_buf.at[k - 1], rs_send.at[k], rs_recv.at[k], "tp", peer)
+        c.start()
+        copies.append(c)
+    total = act[...].astype(F32) + term[my].astype(F32)
+    for k in range(1, n_tp):
+        copies[k - 1].wait_recv()
+        total = total + rs_buf[k - 1].astype(F32)
+    res[...] = total
+    mean_sq = jnp.mean(total * total, axis=-1, keepdims=True)
+    normed[my] = (total * lax.rsqrt(mean_sq + epsilon) * gain[...]).astype(BF)
+    cuts = pieces_of(D)
+    gathers = []
+    for p, (at, end) in enumerate(cuts):
+        cols = pl.ds(at, end - at)
+        for k in range(1, n_tp):
+            peer = lax.rem(my + k, n_tp)
+            mine = normed.at[my, :, cols]
+            c = remote(mine, mine, ag_send.at[p, k], ag_recv.at[p, k], "tp", peer)
+            c.start()
+            gathers.append(c)
+    sends = []
+    for p, (at, end) in enumerate(cuts):
+        cols = pl.ds(at, end - at)
+        for k in range(1, n_tp):
+            gathers[p * (n_tp - 1) + k - 1].wait_recv()
+        tokens = normed[:, :, at:end].reshape(n_tp * chunk, end - at)
+        picked = jnp.dot(route[...], tokens, preferred_element_type=F32)
+        for e in range(EXPERTS):
+            out_buf[e, :, at:end] = picked[e * CAP : (e + 1) * CAP].astype(BF)
+        for k in range(1, n_req):
+            peer = lax.rem(me + k, n_req)
+            c = remote(
+                out_buf.at[peer // split, :, cols],
+                rows.at[me, :, cols],
+                a2a_send.at[p, k],
+                a2a_recv.at[p, k],
+                "req",
+                peer,
+            )
+            c.start()
+            sends.append(c)
+        rows[me, :, at:end] = out_buf[me // split, :, at:end]
+    for c in sends:
+        c.wait_recv()
+    for c in copies + gathers + sends:
+        c.wait_send()
+
+
+def dispatch(term, act, gain, route, n_tp, n_req):
+    T, D = term.shape
+    chunk = T // n_tp
+    vmem = pl.BlockSpec(memory_space=pltpu.VMEM)
+    dma = pltpu.SemaphoreType.DMA
+    rows, normed, res = pl.pallas_call(
+        functools.partial(dispatch_kernel, n_tp, n_req),
+        out_shape=(
+            jax.ShapeDtypeStruct((n_req, CAP, D), BF),
+            jax.ShapeDtypeStruct((n_tp, chunk, D), BF),
+            jax.ShapeDtypeStruct((chunk, D), F32),
+        ),
+        in_specs=[vmem] * 4,
+        out_specs=(vmem, vmem, vmem),
+        scratch_shapes=[
+            pltpu.VMEM((n_tp - 1, chunk, D), BF),
+            pltpu.VMEM((EXPERTS, CAP, D), BF),
+            dma((n_tp,)),
+            dma((n_tp,)),
+            dma((PIECES, n_tp)),
+            dma((PIECES, n_tp)),
+            dma((PIECES, n_req)),
+            dma((PIECES, n_req)),
+        ],
+        compiler_params=pltpu.CompilerParams(
+            collective_id=1, has_side_effects=True, vmem_limit_bytes=VMEM_BYTES
+        ),
+    )(term.reshape(n_tp, chunk, D), act, gain, route)
+    return rows.reshape(n_req * CAP, D), normed.reshape(T, D), res
+
+
+def collect_kernel(
+    n_tp, n_req, part, high, low, res, out, back, moe, rs_buf,
+    a2a_send, a2a_recv, rs_send, rs_recv, ag_send, ag_recv,
+):
+    my, me = lax.axis_index("tp"), lax.axis_index("req")
+    chunk, D = res.shape
+    cuts = pieces_of(D)
+    greet(True, True, n_tp, n_req)
+    arrivals, sums, gathers = [], [[] for _ in cuts], []
+    for p, (at, end) in enumerate(cuts):
+        cols = pl.ds(at, end - at)
+        for k in range(1, n_req):
+            peer = lax.rem(me + k, n_req)
+            c = remote(
+                part.at[peer, :, cols],
+                back.at[me, :, cols],
+                a2a_send.at[p, k],
+                a2a_recv.at[p, k],
+                "req",
+                peer,
+            )
+            c.start()
+            arrivals.append(c)
+    back[me] = part[me]
+
+    def combine(p):
+        at, end = cuts[p]
+        cols = pl.ds(at, end - at)
+        for k in range(1, n_req):
+            arrivals[p * (n_req - 1) + k - 1].wait_recv()
+        x = back[:, :, at:end].astype(F32).reshape(n_req * CAP, end - at).astype(BF)
+        y = jnp.dot(high[...], x, preferred_element_type=F32)
+        y = y + jnp.dot(low[...], x, preferred_element_type=F32)
+        moe[:, :, at:end] = y.astype(BF).reshape(n_tp, chunk, end - at)
+        for k in range(1, n_tp):
+            peer = lax.rem(my + k, n_tp)
+            c = remote(
+                moe.at[peer, :, cols],
+                rs_buf.at[k - 1, :, cols],
+                rs_send.at[p, k],
+                rs_recv.at[p, k],
+                "tp",
+                peer,
+            )
+            c.start()
+            sums[p].append(c)
+
+    def finish(p):
+        at, end = cuts[p]
+        cols = pl.ds(at, end - at)
+        for c in sums[p]:
+            c.wait_recv()
+        y = moe[my, :, at:end].astype(F32)
+        for k in range(1, n_tp):
+            y = y + rs_buf[k - 1, :, at:end].astype(F32)
+        out[my, :, at:end] = (res[:, at:end] + y).astype(BF)
+        for k in range(1, n_tp):
+            peer = lax.rem(my + k, n_tp)
+            mine = out.at[my, :, cols]
+            c = remote(mine, mine, ag_send.at[p, k], ag_recv.at[p, k], "tp", peer)
+            c.start()
+            gathers.append(c)
+
+    for p in range(len(cuts)):
+        combine(p)
+        if p > 0:
+            finish(p - 1)
+    finish(len(cuts) - 1)
+    for c in gathers:
+        c.wait_recv()
+    for c in arrivals + sum(sums, []) + gathers:
+        c.wait_send()
+
+
+def collect(part, high, low, res, n_tp, n_req):
+    chunk, D = res.shape
+    vmem = pl.BlockSpec(memory_space=pltpu.VMEM)
+    dma = pltpu.SemaphoreType.DMA
+    out = pl.pallas_call(
+        functools.partial(collect_kernel, n_tp, n_req),
+        out_shape=jax.ShapeDtypeStruct((n_tp, chunk, D), BF),
+        in_specs=[vmem] * 4,
+        out_specs=vmem,
+        scratch_shapes=[
+            pltpu.VMEM((n_req, CAP, D), BF),
+            pltpu.VMEM((n_tp, chunk, D), BF),
+            pltpu.VMEM((n_tp - 1, chunk, D), BF),
+            dma((PIECES, n_req)),
+            dma((PIECES, n_req)),
+            dma((PIECES, n_tp)),
+            dma((PIECES, n_tp)),
+            dma((PIECES, n_tp)),
+            dma((PIECES, n_tp)),
+        ],
+        compiler_params=pltpu.CompilerParams(
+            collective_id=2, has_side_effects=True, vmem_limit_bytes=VMEM_BYTES
+        ),
+    )(part.reshape(n_req, CAP, D), high, low, res)
+    return out.reshape(n_tp * chunk, D)
 
 
 def per_device(
@@ -120,8 +370,10 @@
         axis=0,
         tiled=True,
     )[:, :, :width]
-    pool_exp = lax.all_gather(down_t[:, 3 * R :], "req", axis=0, tiled=True)
-    pool_bup = lax.all_gather(pool_bout, "req", axis=0, tiled=True)
+    pool_late = lax.all_gather(
+        jnp.concatenate([down_t[:, 3 * R :], pool_bout], axis=1), "req", axis=0, tiled=True
+    )
+    pool_exp, pool_bup = pool_late[:, :R], pool_late[:, R:]
 
     row = lengths[0]
     n_in = row.shape[0]
@@ -171,7 +423,7 @@
     ).reshape(3 * R, n_slots, T)
     slot_row = coeff_mask.T
     coeff_part = jnp.sum(jnp.where(slot_row[None], down_all, 0.0), axis=1)
-    coeff = lax.psum(coeff_part, "tp").astype(BF)
+    coeff = small_sum(coeff_part, n_tp).astype(BF)
 
     projected = []
     for p in range(3):
@@ -232,16 +484,10 @@
 
     aout_all = dot_nt(attended, pool_up[:, 3 * R :].reshape(n_slots * R, width))
     spread_hi, spread_lo = split_two(jnp.where(mask_r, adapter_scale * aout_all, 0.0))
-    cuts = pieces_of(D)
     bup = pool_bup.reshape(n_slots * R, D)
-    mixed = []
-    for at, end in cuts:
-        term = (
-            dot(attended, output_weight[:, at:end])
-            + dot(spread_hi, bup[:, at:end])
-            + dot(spread_lo, bup[:, at:end])
-        )
-        mixed.append(sum_tp(term.astype(BF), mixed))
+    term = dot(attended, output_weight) + dot(
+        jnp.concatenate([spread_hi, spread_lo], axis=1), jnp.concatenate([bup, bup], axis=0)
+    )
 
     split = n_req // EXPERTS
     experts = [experts_of[:, k : k + 1] for k in range(2)]
@@ -264,43 +510,30 @@
         return got.reshape(n_req * CAP, x.shape[1])
 
     units = w_gate_up.shape[3]
-    residual = []
-    pre = []
-    before_act = None
-    square = 0.0
-    for (at, end), mix in zip(cuts, mixed):
-        res = act[:, at:end] + mix.astype(F32)
-        residual.append(res)
-        square = square + jnp.sum(res * res, axis=-1, keepdims=True)
-        pre_p = (res * moe_gain[None, at:end]).astype(BF)
-        pre.append(pre_p)
-        rows = send(pre_p)
-        gu = w_gate_up[0, at:end].reshape(end - at, 2 * units)
-        part = dot(rows, gu)
-        before_act = part if before_act is None else before_act + part
-    scale = lax.rsqrt(square / D + epsilon)
-    exp_all = 0.0
-    logits = 0.0
-    pool_exp = pool_exp.reshape(n_slots * R, D)
-    for (at, end), pre_p in zip(cuts, pre):
-        exp_all = exp_all + dot_nt(pre_p, pool_exp[:, at:end])
-        logits = logits + dot(pre_p, router[at:end])
-    logits = logits * scale
-    coeff_exp = jnp.where(mask_r, exp_all * scale, 0.0).astype(BF)
+    chunk = T // n_tp
+    rows, normed_moe, res = dispatch(
+        term.astype(BF),
+        lax.dynamic_slice_in_dim(activations, my_tp * chunk, chunk, 0),
+        moe_gain[None],
+        route.T,
+        n_tp,
+        n_req,
+    )
+    exp_all = dot_nt(normed_moe, pool_exp.reshape(n_slots * R, D))
+    logits = dot(normed_moe, router)
+    coeff_exp = jnp.where(mask_r, exp_all, 0.0).astype(BF)
     fold = (iota((n_slots * R, R), 0) % R == iota((n_slots * R, R), 1)).astype(BF)
     coeff_exp = dot(coeff_exp, fold).astype(BF)
-    scale_hi, scale_lo = split_two(scale)
-    meta = jnp.concatenate([coeff_exp, adapter.astype(BF), scale_hi, scale_lo], axis=1)
+    meta = jnp.concatenate([coeff_exp, adapter.astype(BF)], axis=1)
     got = send(meta)
     got_coeff = got[:, :R]
     got_ids = got[:, R : R + 1].astype(jnp.int32)
-    got_scale = got[:, R + 1 : R + 2].astype(F32) + got[:, R + 2 : R + 3].astype(F32)
     unfold = (iota((R, n_adapters * R), 1) % R == iota((R, n_adapters * R), 0)).astype(BF)
     broad = dot(got_coeff * jnp.array(adapter_scale, BF), unfold)
     broad = jnp.where(
         got_ids == iota((n_req * CAP, n_adapters * R), 1) // R, broad, 0.0
     ).astype(BF)
-    before_act = before_act * got_scale + dot(
+    before_act = dot(rows, w_gate_up[0].reshape(D, 2 * units)) + dot(
         broad, expert_up_factors[0].reshape(n_adapters * R, 2 * units)
     )
     hidden = (jax.nn.silu(before_act[:, :units]) * before_act[:, units:]).astype(BF)
@@ -315,16 +548,8 @@
     ).reshape(T, n_req * CAP)
     combine_hi, combine_lo = split_two(combine)
 
-    outs, moe_sums = [], []
-    for (at, end), res in zip(cuts, residual):
-        part = dot(hidden, w_down[0][:, at:end]).astype(BF)
-        back = lax.all_to_all(
-            part.reshape(n_req, CAP, end - at), "req", split_axis=0, concat_axis=0, tiled=True
-        ).reshape(n_req * CAP, end - at)
-        moe = dot(combine_hi, back) + dot(combine_lo, back)
-        moe_sums.append(sum_tp(moe.astype(BF), moe_sums))
-        outs.append((res + moe_sums[-1].astype(F32)).astype(BF))
-    layer_out = jnp.concatenate(outs, axis=1)
+    part = dot(hidden, w_down[0]).astype(BF)
+    layer_out = collect(part, combine_hi, combine_lo, res, n_tp, n_req)
     return (layer_out, page_cache)
 
 

time: 402 us -> 282 us (0.70)
  waiting for transfers between devices: 194 us -> 0.04 us
  Pallas kernels: 0 us -> 148 us
  matrix products: 91.2 us -> 59 us
  blocking collectives: 33.6 us -> 13.3 us
  starting transfers between devices: 21.4 us -> 4.8 us
  other arithmetic: 22.2 us -> 13 us
    pallas_call x0 -> x3, Pallas kernels: none -> 148 us  [the longest x1 71.8 us: collect(): pl.pallas_call(functools.partial(collect_kernel, n_tp, n_req), out_shape=...]
    psum x4 -> x0, waiting for transfers between devices: 128 us -> none  [sum_tp(): return lax.psum(x, 'tp')]
    dot_general x19 -> x8, matrix products: 65.6 us -> 35.6 us  [dot(): return jnp.dot(a, b, preferred_element_type=F32)]
    all_to_all x2 -> x0, waiting for transfers between devices: 24.5 us -> none  [per_device(): lax.all_to_all(part.reshape(n_req, CAP, end - at), 'req', split_axis=0, c...]
    all_gather x2 -> x1, waiting for transfers between devices: 23.8 us -> 0.01 us  [per_device(): lax.all_gather(jnp.concatenate([down_t[:, 3 * R:], pool_bout], axis=1), '...]
    psum x1 -> x0, blocking collectives: 19.3 us -> none  [per_device(): coeff = lax.psum(coeff_part, 'tp').astype(BF)]
    all_to_all x3 -> x1, waiting for transfers between devices: 16.2 us -> 0.01 us  [send(): lax.all_to_all(rows.reshape(n_req, CAP, x.shape[1]), 'req', split_axis=0,...]
    all_to_all x2 -> x0, starting transfers between devices: 9.02 us -> none  [per_device(): lax.all_to_all(part.reshape(n_req, CAP, end - at), 'req', split_axis=0, c...]
  transfers between devices with their start and end apart: 12 -> 3, of which waited for: 10 -> 0; matrix products, arithmetic and copies ran while one was open for 23% -> 24% of each run, Pallas kernels for 0% -> 3%
where the time goes in v2:
time: 282 us; the launch traced here: 278 us
  Pallas kernels  148 us (52%)
  matrix products  59 us (21%)
  local copies, waits for them, and re-layouts  24.4 us (9%)
  between operations  14.9 us (5%)
  blocking collectives  13.3 us (5%)
  other arithmetic  13 us (5%)
  starting transfers between devices  4.8 us (2%)
    pallas_call x1, Pallas kernels, collect(): pl.pallas_call(functools.partial(collect_kernel, n_tp, n_req), out_shape=...  71.8 us
    pallas_call x1, Pallas kernels, dispatch(): pl.pallas_call(functools.partial(dispatch_kernel, n_tp, n_req), out_shape...  67.8 us
    dot_general x8, matrix products, dot(): return jnp.dot(a, b, preferred_element_type=F32)  35.6 us
    all_gather x1, blocking collectives, per_device(): lax.all_gather(jnp.pad(down_part, ((0, 0), (0, 0), (0, pad))), 'req', axi...  13.3 us
    unnamed x109, local copies, waits for them, and re-layouts  10.8 us
    dot_general x5, matrix products, dot_nt(): lax.dot_general(a, b, (((1,), (1,)), ((), ())), preferred_element_type=F32)  9.4 us
    pallas_call x1, Pallas kernels, small_sum(): pl.pallas_call(functools.partial(small_sum_kernel, n_tp), out_shape=jax.S...  8.79 us
  transfers between devices with their start and end apart: 3, of which 0 were waited for; matrix products, arithmetic and copies ran while one was open for 24% of the time, Pallas kernels for 3%

profile of v2, /device:TPU:0, one launch (start us, length us, event | category | flops | bytes accessed | tf_op | source)
XLA Modules:
  0.0 277.9 jit_solution(11800589537528031907)
XLA Ops:
  7.3 1.8 fusion.93
  10.1 1.7 pad_maximum_fusion.1
  18.3 2.4 copy.54
  21.8 13.3 %all_gather.10 = bf16[16,48,640]{2,1,0:T(8,128)(2,1)S(1)} all-gather(bf16[2,48,640]{2,1,0:T(8,128)(2,1)S(1)} %pad.9), channel_id=1, replica_groups=mesh['req'=8,'tp'=4] {'req'}, dimensions={0}, use_global_device_ids=true | all-gather | bytes 1105920 | tf_op jit(solution)/shard_map/all_gather | solution.py:364
  36.4 8.8 %shard_map.194 = f32[48,256]{1,0:T(8,128)S(1)} custom-call(f32[48,256]{1,0:T(8,128)S(1)} %fusion.49.x_ref), custom_call_target="tpu_custom_call" | custom-call | tf_op jit(solution)/shard_map/pallas_call | solution.py:119
  48.2 2.7 fusion.36
  52.5 2.2 copy.60
  56.1 2.6 fusion.45
  60.9 2.2 copy.61
  63.1 3.1 %pad_maximum_fusion = bf16[6,128,2,576]{3,1,0,2:T(8,128)(2,1)} fusion(bf16[6,128,1,576]{3,1,0,2:T(8,128)(2,1)} %bitcast.132, bf16[6,128,1,576]{3,1,0,2:T(8,128)(2,1)} %bitcast.131), kind=kLoop, calls=%fused_computation.31 | loop fusion | flops 884736 | bytes 3538944 | tf_op jit(solution)/shard_map/stack | solution.py:469
  66.2 3.9 %copy.62 = bf16[6,128,2,576]{1,3,2,0:T(8,128)(2,1)} copy(bf16[6,128,2,576]{3,1,0,2:T(8,128)(2,1)} %pad_maximum_fusion) | data formatting | bytes 3538944
  70.1 1.8 slice.130
  73.2 2.6 fusion.39
  76.7 4.0 %fusion.160 = (f32[9,256]{1,0:T(8,128)}, f32[9,256,256]{1,2,0:T(8,128)}) fusion(pred[256,256]{0,1:T(8,128)(4,1)} %fusion.88, bf16[9,32,256]{2,1,0:T(8,128)(2,1)} %get-tuple-element.27, bf16[9,32,256]{2,1,0:T(8,128)(2,1)} %get-tuple-element.26, bf16[9,32,256]{2,1,0:T(8,128)(2,1)S(1)} %get-tuple-element.29, bf16[9,32,256]{2,1,0:T(8,128)(2,1)S(1)} %get-tuple-element.28), kind=kOutput, calls=%fused_computation.230 | convolution fusion | flops 79036672 | bytes 3023872 | tf_op jit(solution)/shard_map/sub | solution.py:477
  80.7 2.1 convolution_convert_fusion.2
  83.8 2.8 %fusion.157 = (bf16[16,16,2304]{2,1,0:T(8,128)(2,1)}, bf16[16,16,2304]{2,1,0:T(8,128)(2,1)S(1)}) fusion(bf16[16,32,2304]{2,1,0:T(8,128)(2,1)} %all-gather.5.cloned.1.call-done), kind=kLoop, calls=%fused_computation.227 | loop fusion | bytes 4718592 | tf_op jit(solution)/shard_map/slice | solution.py:376
  88.6 67.8 %shard_map.195 = (bf16[8,72,2304]{2,1,0:T(8,128)(2,1)S(1)}, bf16[4,64,2304]{2,1,0:T(8,128)(2,1)S(1)}, f32[64,2304]{1,0:T(8,128)S(1)}) custom-call(bf16[4,64,2304]{2,1,0:T(8,128)(2,1)S(1)} %bitcast.125, bf16[64,2304]{1,0:T(8,128)(2,1)S(1)} %constant_dynamic-slice_fusion.act, f32[1,2304]{1,0:T(1,128)S(1)} %broadcast_in_dim.227.gain, ...), custom_call_target="tpu_custom_call" | custom-call | tf_op jit(solution)/shard_map/pallas_call | solution.py:199
  156.5 1.6 copy-done.4
  158.6 1.9 fusion.57
  161.8 4.7 %all-to-all-start = ((bf16[8,2,612]{2,1,0:T(2,128)(2,1)}), bf16[8,2,612]{2,1,0:T(2,128)(2,1)S(1)}, u32[]{:S(2)}, u32[]{:S(2)}) async-start(bf16[8,2,612]{2,1,0:T(2,128)(2,1)} %reshape.318), calls=%async_computation | async-start | bytes 40960 | tf_op jit(solution)/shard_map/all_to_all | solution.py:507
  166.6 14.2 %fusion.163 = f32[576,2880]{1,0:T(8,128)} fusion(bf16[576,2304]{1,0:T(8,128)(2,1)} %bitcast.130, bf16[2304,2880]{0,1:T(8,128)(2,1)} %bitcast.166), kind=kOutput, calls=%fused_computation.232 | convolution fusion | flops 7644119040 | bytes 22560768 | tf_op jit(solution)/shard_map/dot_general | solution.py:34
  181.3 7.0 %convolution_add_fusion = f32[576,2880]{1,0:T(8,128)} fusion(f32[576,2880]{1,0:T(8,128)} %fusion.163, bf16[256,2880]{0,1:T(8,128)(2,1)S(1)} %bitcast.133, s32[256]{0:T(256)S(1)} %copy-done.31, s32[256]{0:T(256)S(1)} %copy-done.33, s32[576]{0:T(1024)S(1)} %fusion.133, pred[256]{0:T(512)(128)(4,1)S(1)} %copy-done.43, bf16[576,17]{0,1:T(8,128)(2,1)S(1)} %reshape.309, ...), kind=kOutput, calls=%fused_computation.3 | convolution fusion | flops 856331264 | bytes 14775296 | tf_op jit(solution)/shard_map/dot_general | solution.py:34
  188.4 9.8 %fusion.3 = bf16[576,2304]{1,0:T(8,128)(2,1)S(1)} fusion(bf16[1,1440,2304]{2,1,0:T(8,128)(2,1)} %param.31, f32[576,2880]{1,0:T(8,128)} %convolution_add_fusion), kind=kOutput, calls=%fused_computation.4 | convolution fusion | flops 3828363264 | bytes 16367616 | tf_op jit(solution)/shard_map/dot_general | solution.py:34
  198.2 71.8 %shard_map.196 = bf16[4,64,2304]{2,1,0:T(8,128)(2,1)S(1)} custom-call(bf16[8,72,2304]{2,1,0:T(8,128)(2,1)S(1)} %bitcast.127, bf16[256,576]{1,0:T(8,128)(2,1)S(1)} %get-tuple-element.38.high, bf16[256,576]{1,0:T(8,128)(2,1)S(1)} %get-tuple-element.37.low, f32[64,2304]{1,0:T(8,128)S(1)} %copy-done.3), custom_call_target="tpu_custom_call" | custom-call | tf_op jit(solution)/shard_map/pallas_call | solution.py:303
  (169 shorter events, 26.1 us)
Async XLA Ops:
  7.2 80.2 %copy-start = (bf16[576,2304]{1,0:T(8,128)(2,1)S(1)}, bf16[576,2304]{1,0:T(8,128)(2,1)}, u32[]{:S(2)}) copy-start(bf16[576,2304]{1,0:T(8,128)(2,1)} %param.28) | copy-start | bytes 7962628
  7.2 10.2 %copy-start.17 = (bf16[256,64]{1,0:T(8,128)(2,1)S(1)}, bf16[256,64]{1,0:T(8,128)(2,1)}, u32[]{:S(2)}) copy-start(bf16[256,64]{1,0:T(8,128)(2,1)} %constant.159) | copy-start | bytes 98308
  7.3 39.4 %all-gather.3.cloned.1.call-start = ((), (), s32[]{:S(2)}) async-start(), calls=%async_computation.1 | async-start | bytes 1474560 | tf_op jit(solution)/shard_map/all_gather | solution.py:367
  9.1 74.6 %all-gather.5.cloned.1.call-start = ((), (), s32[]{:S(2)}) async-start(), calls=%async_computation.2 | async-start | bytes 2654208 | tf_op jit(solution)/shard_map/all_gather | solution.py:373
  14.9 20.3 %copy-start.39 = (s32[256]{0:T(256)}, s32[256]{0:T(256)S(1)}, u32[]{:S(2)}) copy-start(s32[256]{0:T(256)S(1)} %get-tuple-element.23) | copy-start | bytes 3076
  16.8 29.1 %copy-start.34 = (s32[256,1]{0,1:T(1,128)}, s32[256,1]{0,1:T(1,128)S(1)}, u32[]{:S(2)}) copy-start(s32[256,1]{0,1:T(1,128)S(1)} %get-tuple-element.43) | copy-start | bytes 3076
  16.8 29.1 %copy-start.36 = (s32[256,1]{0,1:T(1,128)}, s32[256,1]{0,1:T(1,128)S(1)}, u32[]{:S(2)}) copy-start(s32[256,1]{0,1:T(1,128)S(1)} %get-tuple-element.44) | copy-start | bytes 3076
  16.8 29.9 %copy-start.38 = (pred[16,256]{1,0:T(8,128)(4,1)}, pred[16,256]{1,0:T(8,128)(4,1)S(1)}, u32[]{:S(2)}) copy-start(pred[16,256]{1,0:T(8,128)(4,1)S(1)} %iota_compare_fusion.19) | copy-start | bytes 12292
  18.3 17.2 %copy-start.21 = (f32[2304]{0:T(1024)S(1)}, f32[2304]{0:T(1024)}, u32[]{:S(2)}) copy-start(f32[2304]{0:T(1024)} %param.25) | copy-start | bytes 27652
  21.7 13.5 %copy-start.5 = (bf16[256,2304]{0,1:T(8,128)(2,1)S(1)}, bf16[256,2304]{0,1:T(8,128)(2,1)}, u32[]{:S(2)}) copy-start(bf16[256,2304]{0,1:T(8,128)(2,1)} %copy.54) | copy-start | bytes 3538948
  35.9 10.2 %copy-start.7 = (bf16[256,2304]{0,1:T(8,128)(2,1)}, bf16[256,2304]{0,1:T(8,128)(2,1)S(1)}, u32[]{:S(2)}) copy-start(bf16[256,2304]{0,1:T(8,128)(2,1)S(1)} %fusion.19) | copy-start | bytes 3538948
  87.4 70.7 %copy-start.20 = (bf16[2304,8]{0,1:T(8,128)(2,1)S(1)}, bf16[2304,8]{0,1:T(8,128)(2,1)}, u32[]{:S(2)}) copy-start(bf16[2304,8]{0,1:T(8,128)(2,1)} %param.29) | copy-start | bytes 110596
  87.4 70.7 %copy-start.35 = (s32[256,1]{0,1:T(1,128)S(1)}, s32[256,1]{0,1:T(1,128)}, u32[]{:S(2)}) copy-start(s32[256,1]{0,1:T(1,128)} %copy-done.34) | copy-start | bytes 3076
  87.4 70.7 %copy-start.37 = (s32[256,1]{0,1:T(1,128)S(1)}, s32[256,1]{0,1:T(1,128)}, u32[]{:S(2)}) copy-start(s32[256,1]{0,1:T(1,128)} %copy-done.36) | copy-start | bytes 3076
  88.6 70.0 %copy-start.28 = (s32[256]{0:T(256)S(1)}, s32[256]{0:T(256)}, u32[]{:S(2)}) copy-start(s32[256]{0:T(256)} %get-tuple-element.53) | copy-start | bytes 3076
  88.6 70.0 %copy-start.29 = (s32[256]{0:T(256)S(1)}, s32[256]{0:T(256)}, u32[]{:S(2)}) copy-start(s32[256]{0:T(256)} %get-tuple-element.54) | copy-start | bytes 3076
  88.6 70.0 %copy-start.31 = (s32[256]{0:T(256)S(1)}, s32[256]{0:T(256)}, u32[]{:S(2)}) copy-start(s32[256]{0:T(256)} %get-tuple-element.51) | copy-start | bytes 3076
  88.6 70.0 %copy-start.33 = (s32[256]{0:T(256)S(1)}, s32[256]{0:T(256)}, u32[]{:S(2)}) copy-start(s32[256]{0:T(256)} %get-tuple-element.52) | copy-start | bytes 3076
  88.6 70.0 %copy-start.41 = (s32[256]{0:T(256)S(1)}, s32[256]{0:T(256)}, u32[]{:S(2)}) copy-start(s32[256]{0:T(256)} %copy-done.39) | copy-start | bytes 3076
  88.6 70.0 %copy-start.43 = (pred[256]{0:T(512)(128)(4,1)S(1)}, pred[256]{0:T(512)(128)(4,1)}, u32[]{:S(2)}) copy-start(pred[256]{0:T(512)(128)(4,1)} %compare_and_fusion.1) | copy-start | bytes 772
  88.6 70.0 %copy-start.44 = (pred[256]{0:T(512)(128)(4,1)S(1)}, pred[256]{0:T(512)(128)(4,1)}, u32[]{:S(2)}) copy-start(pred[256]{0:T(512)(128)(4,1)} %compare_and_fusion) | copy-start | bytes 772
  161.8 19.2 %all-to-all-start = ((bf16[8,2,612]{2,1,0:T(2,128)(2,1)}), bf16[8,2,612]{2,1,0:T(2,128)(2,1)S(1)}, u32[]{:S(2)}, u32[]{:S(2)}) async-start(bf16[8,2,612]{2,1,0:T(2,128)(2,1)} %reshape.318), calls=%async_computation | async-start | bytes 40960 | tf_op jit(solution)/shard_map/all_to_all | solution.py:507
  166.6 14.8 %copy-start.6 = (bf16[1,256,2,1440]{1,3,2,0:T(8,128)(2,1)S(1)}, bf16[1,256,2,1440]{1,3,2,0:T(8,128)(2,1)}, u32[]{:S(2)}) copy-start(bf16[1,256,2,1440]{1,3,2,0:T(8,128)(2,1)} %param.32) | copy-start | bytes 4423684
  198.2 72.9 %copy-start.1 = (bf16[576,2304]{1,0:T(8,128)(2,1)S(1)}, bf16[576,2304]{1,0:T(8,128)(2,1)}, u32[]{:S(2)}) copy-start(bf16[576,2304]{1,0:T(8,128)(2,1)} %param.28) | copy-start | bytes 7962628
  (31 other events, 133.2 us)
Sparse Core Ops, SparseCore 0:
  10.6 27.7 all-gather.2
  40.3 29.3 all-gather.4

commit v3 on v2

--- a/solution.py
+++ b/solution.py
@@ -16,7 +16,7 @@
 CAP = 72
 PIECES = 3
 MESH = pl.DeviceIdType.MESH
-VMEM_BYTES = 44 * 2**20
+VMEM_BYTES = 20 * 2**20
 
 epsilon = 1e-05
 adapter_scale = 2.0
@@ -458,15 +458,17 @@
     values = projected[2].astype(BF).reshape(heads, HEAD_SIZE, T)
 
     place_hot = (cache_row == iota((T, n_pages * PAGE), 1)).astype(BF)
-    cache = [
+    key_value = jnp.concatenate([keys.reshape(width, T), values.reshape(width, T)], axis=0)
+    page_cache = (
         lax.dot_general(
-            place_hot, x.reshape(width, T), (((0,), (1,)), ((), ())), preferred_element_type=F32
+            place_hot.T.reshape(n_pages, PAGE, T),
+            key_value,
+            (((2,), (1,)), ((), ())),
+            preferred_element_type=F32,
         )
         .astype(BF)
-        .reshape(n_pages, PAGE, width)
-        for x in (keys, values)
-    ]
-    page_cache = jnp.stack(cache, axis=2)
+        .reshape(n_pages, PAGE, 2, width)
+    )
 
     scores = jnp.einsum("hdq,hdk->hqk", queries, keys, preferred_element_type=F32) * (
         1.0 / math.sqrt(HEAD_SIZE)
@@ -529,11 +531,11 @@
     got_coeff = got[:, :R]
     got_ids = got[:, R : R + 1].astype(jnp.int32)
     unfold = (iota((R, n_adapters * R), 1) % R == iota((R, n_adapters * R), 0)).astype(BF)
-    broad = dot(got_coeff * jnp.array(adapter_scale, BF), unfold)
+    broad = dot(got_coeff, unfold)
     broad = jnp.where(
         got_ids == iota((n_req * CAP, n_adapters * R), 1) // R, broad, 0.0
     ).astype(BF)
-    before_act = dot(rows, w_gate_up[0].reshape(D, 2 * units)) + dot(
+    before_act = dot(rows, w_gate_up[0].reshape(D, 2 * units)) + adapter_scale * dot(
         broad, expert_up_factors[0].reshape(n_adapters * R, 2 * units)
     )
     hidden = (jax.nn.silu(before_act[:, :units]) * before_act[:, units:]).astype(BF)

time: 282 us -> 276 us (0.979)
  local copies, waits for them, and re-layouts: 24.4 us -> 21.4 us
    another operation x2 -> x1, other arithmetic: 3.87 us -> 0.8 us  [the longest x1 3.07 us: per_device(): page_cache = jnp.stack(cache, axis=2)]
    unnamed x109 -> x112, local copies, waits for them, and re-layouts: 10.8 us -> 8.33 us
  transfers between devices with their start and end apart: 3 -> 3, of which waited for: 0 -> 0; matrix products, arithmetic and copies ran while one was open for 24% -> 22% of each run, Pallas kernels for 3% -> 3%
where the time goes in v3:
time: 276 us; the launch traced here: 272 us
  Pallas kernels  147 us (53%)
  matrix products  57.9 us (21%)
  local copies, waits for them, and re-layouts  21.4 us (8%)
  between operations  14.9 us (5%)
  blocking collectives  14.8 us (5%)
  other arithmetic  12.7 us (5%)
  starting transfers between devices  3.64 us (1%)
    pallas_call x1, Pallas kernels, collect(): pl.pallas_call(functools.partial(collect_kernel, n_tp, n_req), out_shape=...  71.6 us
    pallas_call x1, Pallas kernels, dispatch(): pl.pallas_call(functools.partial(dispatch_kernel, n_tp, n_req), out_shape...  67.2 us
    dot_general x8, matrix products, dot(): return jnp.dot(a, b, preferred_element_type=F32)  35.6 us
    all_gather x1, blocking collectives, per_device(): lax.all_gather(jnp.pad(down_part, ((0, 0), (0, 0), (0, pad))), 'req', axi...  14.8 us
    dot_general x5, matrix products, dot_nt(): lax.dot_general(a, b, (((1,), (1,)), ((), ())), preferred_element_type=F32)  9.33 us
    unnamed x112, local copies, waits for them, and re-layouts  8.33 us
    pallas_call x1, Pallas kernels, small_sum(): pl.pallas_call(functools.partial(small_sum_kernel, n_tp), out_shape=jax.S...  8.14 us
  transfers between devices with their start and end apart: 3, of which 0 were waited for; matrix products, arithmetic and copies ran while one was open for 22% of the time, Pallas kernels for 3%

profile of v3, /device:TPU:0, one launch (start us, length us, event | category | flops | bytes accessed | tf_op | source)
XLA Modules:
  0.0 272.3 jit_solution(8117358167724898748)
XLA Ops:
  7.3 1.8 fusion.96
  10.1 1.7 pad_maximum_fusion
  18.0 14.8 %all_gather.10 = bf16[16,48,640]{2,1,0:T(8,128)(2,1)} all-gather(bf16[2,48,640]{2,1,0:T(8,128)(2,1)S(1)} %pad.9), channel_id=1, replica_groups=mesh['req'=8,'tp'=4] {'req'}, dimensions={0}, use_global_device_ids=true | all-gather | bytes 1105920 | tf_op jit(solution)/shard_map/all_gather | solution.py:364
  32.8 2.4 copy.47
  35.2 1.7 fusion.17
  36.9 1.7 fusion.19
  40.1 8.1 %shard_map.194 = f32[48,256]{1,0:T(8,128)S(1)} custom-call(f32[48,256]{1,0:T(8,128)S(1)} %fusion.49.x_ref), custom_call_target="tpu_custom_call" | custom-call | tf_op jit(solution)/shard_map/pallas_call | solution.py:119
  53.4 2.6 fusion.36
  57.4 2.6 fusion.45
  60.8 1.9 convolution_convert_fusion
  62.7 3.8 %copy.53 = bf16[6,128,1152]{1,2,0:T(8,128)(2,1)} copy(bf16[6,128,1152]{2,1,0:T(8,128)(2,1)} %convolution_convert_fusion) | data formatting | bytes 3538944 | tf_op jit(solution)/shard_map/convert_element_type | solution.py:469
  66.6 1.8 slice.130
  69.7 2.6 fusion.39
  73.1 4.0 %fusion.162 = (f32[9,256]{1,0:T(8,128)}, f32[9,256,256]{1,2,0:T(8,128)}) fusion(pred[256,256]{0,1:T(8,128)(4,1)} %fusion.91, bf16[9,32,256]{2,1,0:T(8,128)(2,1)} %get-tuple-element.21, bf16[9,32,256]{2,1,0:T(8,128)(2,1)} %get-tuple-element.20, bf16[9,32,256]{2,1,0:T(8,128)(2,1)S(1)} %get-tuple-element.23, bf16[9,32,256]{2,1,0:T(8,128)(2,1)S(1)} %get-tuple-element.22), kind=kOutput, calls=%fused_computation.231 | convolution fusion | flops 79036672 | bytes 3023872 | tf_op jit(solution)/shard_map/sub | solution.py:479
  77.1 2.1 convolution_convert_fusion.1
  80.2 2.8 %fusion.159 = (bf16[16,16,2304]{2,1,0:T(8,128)(2,1)}, bf16[16,16,2304]{2,1,0:T(8,128)(2,1)S(1)}) fusion(bf16[16,32,2304]{2,1,0:T(8,128)(2,1)} %all-gather.5.cloned.1.call-done), kind=kLoop, calls=%fused_computation.228 | loop fusion | bytes 4718592 | tf_op jit(solution)/shard_map/slice | solution.py:376
  85.1 67.2 %shard_map.195 = (bf16[8,72,2304]{2,1,0:T(8,128)(2,1)S(1)}, bf16[4,64,2304]{2,1,0:T(8,128)(2,1)S(1)}, f32[64,2304]{1,0:T(8,128)S(1)}) custom-call(bf16[4,64,2304]{2,1,0:T(8,128)(2,1)S(1)} %bitcast.125, bf16[64,2304]{1,0:T(8,128)(2,1)S(1)} %constant_dynamic-slice_fusion.act, f32[1,2304]{1,0:T(1,128)S(1)} %broadcast_in_dim.227.gain, ...), custom_call_target="tpu_custom_call" | custom-call | tf_op jit(solution)/shard_map/pallas_call | solution.py:199
  152.3 1.6 copy-done.4
  154.4 1.9 fusion.57
  157.6 3.6 %all-to-all-start = ((bf16[8,2,612]{2,1,0:T(2,128)(2,1)}), bf16[8,2,612]{2,1,0:T(2,128)(2,1)S(1)}, u32[]{:S(2)}, u32[]{:S(2)}) async-start(bf16[8,2,612]{2,1,0:T(2,128)(2,1)} %reshape.338), calls=%async_computation | async-start | bytes 40960 | tf_op jit(solution)/shard_map/all_to_all | solution.py:509
  161.2 14.3 %fusion.165 = f32[576,2880]{1,0:T(8,128)} fusion(bf16[576,2304]{1,0:T(8,128)(2,1)} %bitcast.130, bf16[2304,2880]{0,1:T(8,128)(2,1)} %bitcast.165), kind=kOutput, calls=%fused_computation.233 | convolution fusion | flops 7644119040 | bytes 22560768 | tf_op jit(solution)/shard_map/dot_general | solution.py:34
  176.0 7.0 %multiply_add_fusion = f32[576,2880]{1,0:T(8,128)} fusion(f32[576,2880]{1,0:T(8,128)} %fusion.165, bf16[256,2880]{0,1:T(8,128)(2,1)S(1)} %bitcast.132, s32[256]{0:T(256)S(1)} %copy-done.30, s32[256]{0:T(256)S(1)} %copy-done.32, s32[576]{0:T(1024)S(1)} %fusion.136, pred[256]{0:T(512)(128)(4,1)S(1)} %copy-done.45, bf16[576,17]{0,1:T(8,128)(2,1)S(1)} %reshape.327, ...), kind=kOutput, calls=%fused_computation.1 | convolution fusion | flops 857980928 | bytes 14775296 | tf_op jit(solution)/shard_map/dot_general | solution.py:34
  183.0 9.8 %fusion.3 = bf16[576,2304]{1,0:T(8,128)(2,1)S(1)} fusion(bf16[1,1440,2304]{2,1,0:T(8,128)(2,1)} %param.31, f32[576,2880]{1,0:T(8,128)} %multiply_add_fusion), kind=kOutput, calls=%fused_computation.4 | convolution fusion | flops 3828363264 | bytes 16367616 | tf_op jit(solution)/shard_map/dot_general | solution.py:34
  192.9 71.6 %shard_map.196 = bf16[4,64,2304]{2,1,0:T(8,128)(2,1)S(1)} custom-call(bf16[8,72,2304]{2,1,0:T(8,128)(2,1)S(1)} %bitcast.127, bf16[256,576]{1,0:T(8,128)(2,1)S(1)} %get-tuple-element.32.high, bf16[256,576]{1,0:T(8,128)(2,1)S(1)} %get-tuple-element.31.low, f32[64,2304]{1,0:T(8,128)S(1)} %copy-done.3), custom_call_target="tpu_custom_call" | custom-call | tf_op jit(solution)/shard_map/pallas_call | solution.py:303
  (170 shorter events, 24.1 us)
Async XLA Ops:
  7.2 76.7 %copy-start = (bf16[576,2304]{1,0:T(8,128)(2,1)S(1)}, bf16[576,2304]{1,0:T(8,128)(2,1)}, u32[]{:S(2)}) copy-start(bf16[576,2304]{1,0:T(8,128)(2,1)} %param.28) | copy-start | bytes 7962628
  7.2 9.2 %copy-start.18 = (bf16[256,64]{1,0:T(8,128)(2,1)S(1)}, bf16[256,64]{1,0:T(8,128)(2,1)}, u32[]{:S(2)}) copy-start(bf16[256,64]{1,0:T(8,128)(2,1)} %constant.158) | copy-start | bytes 98308
  7.2 9.5 %copy-start.17 = (bf16[256,64]{1,0:T(8,128)(2,1)S(1)}, bf16[256,64]{1,0:T(8,128)(2,1)}, u32[]{:S(2)}) copy-start(bf16[256,64]{1,0:T(8,128)(2,1)} %constant.159) | copy-start | bytes 98308
  7.2 9.7 %copy-start.16 = (bf16[256,64]{1,0:T(8,128)(2,1)S(1)}, bf16[256,64]{1,0:T(8,128)(2,1)}, u32[]{:S(2)}) copy-start(bf16[256,64]{1,0:T(8,128)(2,1)} %constant.160) | copy-start | bytes 98308
  7.3 44.7 %all-gather.3.cloned.1.call-start = ((), (), s32[]{:S(2)}) async-start(), calls=%async_computation.1 | async-start | bytes 1474560 | tf_op jit(solution)/shard_map/all_gather | solution.py:367
  9.1 71.1 %all-gather.5.cloned.1.call-start = ((), (), s32[]{:S(2)}) async-start(), calls=%async_computation.2 | async-start | bytes 2654208 | tf_op jit(solution)/shard_map/all_gather | solution.py:373
  16.4 32.5 %copy-start.33 = (s32[256,1]{0,1:T(1,128)}, s32[256,1]{0,1:T(1,128)S(1)}, u32[]{:S(2)}) copy-start(s32[256,1]{0,1:T(1,128)S(1)} %get-tuple-element.37) | copy-start | bytes 3076
  16.4 32.5 %copy-start.35 = (s32[256,1]{0,1:T(1,128)}, s32[256,1]{0,1:T(1,128)S(1)}, u32[]{:S(2)}) copy-start(s32[256,1]{0,1:T(1,128)S(1)} %get-tuple-element.38) | copy-start | bytes 3076
  16.4 35.6 %copy-start.38 = (pred[16,256]{1,0:T(8,128)(4,1)}, pred[16,256]{1,0:T(8,128)(4,1)S(1)}, u32[]{:S(2)}) copy-start(pred[16,256]{1,0:T(8,128)(4,1)S(1)} %iota_compare_fusion.16) | copy-start | bytes 12292
  18.0 18.9 %copy-start.20 = (f32[2304]{0:T(1024)S(1)}, f32[2304]{0:T(1024)}, u32[]{:S(2)}) copy-start(f32[2304]{0:T(1024)} %param.25) | copy-start | bytes 27652
  36.9 14.0 %copy-start.21 = (f32[2304]{0:T(1024)S(1)}, f32[2304]{0:T(1024)}, u32[]{:S(2)}) copy-start(f32[2304]{0:T(1024)} %param.26) | copy-start | bytes 27652
  83.9 70.0 %copy-start.19 = (bf16[2304,8]{0,1:T(8,128)(2,1)S(1)}, bf16[2304,8]{0,1:T(8,128)(2,1)}, u32[]{:S(2)}) copy-start(bf16[2304,8]{0,1:T(8,128)(2,1)} %param.29) | copy-start | bytes 110596
  83.9 70.0 %copy-start.34 = (s32[256,1]{0,1:T(1,128)S(1)}, s32[256,1]{0,1:T(1,128)}, u32[]{:S(2)}) copy-start(s32[256,1]{0,1:T(1,128)} %copy-done.33) | copy-start | bytes 3076
  83.9 70.0 %copy-start.36 = (s32[256,1]{0,1:T(1,128)S(1)}, s32[256,1]{0,1:T(1,128)}, u32[]{:S(2)}) copy-start(s32[256,1]{0,1:T(1,128)} %copy-done.35) | copy-start | bytes 3076
  85.1 69.3 %copy-start.28 = (s32[256]{0:T(256)S(1)}, s32[256]{0:T(256)}, u32[]{:S(2)}) copy-start(s32[256]{0:T(256)} %get-tuple-element.47) | copy-start | bytes 3076
  85.1 69.3 %copy-start.29 = (s32[256]{0:T(256)S(1)}, s32[256]{0:T(256)}, u32[]{:S(2)}) copy-start(s32[256]{0:T(256)} %get-tuple-element.48) | copy-start | bytes 3076
  85.1 69.3 %copy-start.32 = (s32[256]{0:T(256)S(1)}, s32[256]{0:T(256)}, u32[]{:S(2)}) copy-start(s32[256]{0:T(256)} %get-tuple-element.46) | copy-start | bytes 3076
  85.1 69.3 %copy-start.43 = (s32[256]{0:T(256)S(1)}, s32[256]{0:T(256)}, u32[]{:S(2)}) copy-start(s32[256]{0:T(256)} %copy-done.41) | copy-start | bytes 3076
  85.1 69.3 %copy-start.45 = (pred[256]{0:T(512)(128)(4,1)S(1)}, pred[256]{0:T(512)(128)(4,1)}, u32[]{:S(2)}) copy-start(pred[256]{0:T(512)(128)(4,1)} %compare_and_fusion.1) | copy-start | bytes 772
  85.1 69.3 %copy-start.46 = (pred[256]{0:T(512)(128)(4,1)S(1)}, pred[256]{0:T(512)(128)(4,1)}, u32[]{:S(2)}) copy-start(pred[256]{0:T(512)(128)(4,1)} %compare_and_fusion) | copy-start | bytes 772
  157.6 18.1 %all-to-all-start = ((bf16[8,2,612]{2,1,0:T(2,128)(2,1)}), bf16[8,2,612]{2,1,0:T(2,128)(2,1)S(1)}, u32[]{:S(2)}, u32[]{:S(2)}) async-start(bf16[8,2,612]{2,1,0:T(2,128)(2,1)} %reshape.338), calls=%async_computation | async-start | bytes 40960 | tf_op jit(solution)/shard_map/all_to_all | solution.py:509
  161.2 14.8 %copy-start.5 = (bf16[1,256,2,1440]{1,3,2,0:T(8,128)(2,1)S(1)}, bf16[1,256,2,1440]{1,3,2,0:T(8,128)(2,1)}, u32[]{:S(2)}) copy-start(bf16[1,256,2,1440]{1,3,2,0:T(8,128)(2,1)} %param.32) | copy-start | bytes 4423684
  183.0 9.8 %copy-start.3 = (f32[64,2304]{1,0:T(8,128)S(1)}, f32[64,2304]{1,0:T(8,128)}, u32[]{:S(2)}) copy-start(f32[64,2304]{1,0:T(8,128)} %copy-done.2) | copy-start | bytes 1769476
  192.9 72.6 %copy-start.1 = (bf16[576,2304]{1,0:T(8,128)(2,1)S(1)}, bf16[576,2304]{1,0:T(8,128)(2,1)}, u32[]{:S(2)}) copy-start(bf16[576,2304]{1,0:T(8,128)(2,1)} %param.28) | copy-start | bytes 7962628
  (33 other events, 106.6 us)
Sparse Core Ops, SparseCore 0:
  10.6 28.4 all-gather.2
  40.9 29.1 all-gather.4
